TPU v7x, 32 devices: a whole 2x2x4 slice. The times are simulated.
32 devices in a mesh: groups: 2 (over y), seq: 4 (over z), head: 2 (over x), pair: 2 (over core).
Axes of the slice: x: 2, y: 2, z: 4, core: 2. Of those that a mesh axis runs over, the one named last changes fastest.
Arguments:
- queries: bfloat16 [8192, 40, 128], P(('groups', 'seq'), ('head', 'pair')), parts along dimension 0, may hold values from -4 to 4
- keys: bfloat16 [8192, 40, 128], P(('groups', 'seq'), ('head', 'pair')), parts along dimension 0, may hold values from -4 to 4
- values: bfloat16 [8192, 40, 128], P(('groups', 'seq'), ('head', 'pair')), parts along dimension 0, may hold values from -4 to 4
- grad_out: bfloat16 [8192, 40, 128], P(('groups', 'seq'), ('head', 'pair')), parts along dimension 0, may hold values from -5 to 5
- fine_out: bfloat16 [8192, 40, 128], P(('groups', 'seq'), ('head', 'pair')), parts along dimension 0, may hold values from -5 to 5
- coarse_out: bfloat16 [8192, 40, 128], P(('groups', 'seq'), ('head', 'pair')), parts along dimension 0, may hold values from -5 to 5
- fine_lse: float32 [40, 8192], P(('head', 'pair'), ('groups', 'seq')), parts along dimension 1, may hold values from 6.5 to 8.5
- coarse_lse: float32 [40, 8192], P(('head', 'pair'), ('groups', 'seq')), parts along dimension 1, may hold values from 5 to 7
- select: int32 [128, 1], P(('groups', 'seq')), parts along dimension 0, may hold values from 0 to 63, as said below
Outputs:
- grad_queries: bfloat16 [8192, 40, 128], P(('groups', 'seq'), ('head', 'pair')), parts along dimension 0
- grad_keys: bfloat16 [8192, 40, 128], P(('groups', 'seq'), ('head', 'pair')), parts along dimension 0
- grad_values: bfloat16 [8192, 40, 128], P(('groups', 'seq'), ('head', 'pair')), parts along dimension 0
- pooled_key_grad: float32 [128, 40, 128], P(('groups', 'seq'), ('head', 'pair')), parts along dimension 0
- pooled_value_grad: float32 [128, 40, 128], P(('groups', 'seq'), ('head', 'pair')), parts along dimension 0
There are 2 independent parts, one for each index of `groups`. A program takes and returns all parts, laid end to end along the dimension named above; each array names one. Nothing has to cross between parts.
Inputs may be any that keep to these rules, and one draw needn't show every extreme that they name: `select`: each entry names a cube outside the query cube's own aligned group of 16 cubes; a query cube's 1 entries are distinct. The query cubes of one aligned group name at most 8 cubes of any one other group, counted with repeats; in every draw 1 group are named exactly 8 times by every other group.
All inputs are finite; a program needn't handle non-finite values.
Results may differ from a plain program's by a relative error of at most 0.017.
Values may be sent and summed in bfloat16 or wider, within the bound.
A program may use at most 256 MiB of HBM per device.

v0:
```python
import jax
import jax.numpy as jnp
from jax import lax
from jax.sharding import PartitionSpec as P


def grads_core(query_x, dout_x, lse_x, delta_x, key_x, value_x, scaling):
    scores = scaling * jnp.einsum(
        "...qhe,...khe->...hqk", query_x, key_x, preferred_element_type=jnp.float32
    )
    probs = jnp.exp(scores - lse_x[..., None])
    probs_low = probs.astype(jnp.bfloat16)
    dprobs = jnp.einsum(
        "...qhe,...khe->...hqk", dout_x, value_x, preferred_element_type=jnp.float32
    )
    dscores = (probs * (dprobs - delta_x[..., None])).astype(jnp.bfloat16)
    grad_q = scaling * jnp.einsum(
        "...hqk,...khe->...qhe", dscores, key_x, preferred_element_type=jnp.float32
    )
    grad_k = scaling * jnp.einsum(
        "...hqk,...qhe->...khe", dscores, query_x, preferred_element_type=jnp.float32
    )
    grad_v = jnp.einsum(
        "...hqk,...qhe->...khe", probs_low, dout_x, preferred_element_type=jnp.float32
    )
    return (grad_q, grad_k, grad_v)


def shards(queries, keys, values, grad_out, fine_out, coarse_out, fine_lse, coarse_lse, select):
    row_count, head_count, head_width = queries.shape
    cube_count, far_count = select.shape
    cube_len = row_count // cube_count
    scaling = head_width ** (-0.5)
    seq_size = lax.axis_size("seq")
    slot_cap = max(2, min(cube_count * far_count // 2, 3 * cube_count * far_count // seq_size))
    slot_total = seq_size * slot_cap
    task_total = cube_count * far_count
    delta_fine = jnp.einsum("the,the->ht", grad_out, fine_out, preferred_element_type=jnp.float32)
    delta_coarse = jnp.einsum(
        "the,the->ht", grad_out, coarse_out, preferred_element_type=jnp.float32
    )
    block_count = max(1, row_count // 512)
    block_rows = row_count // block_count

    def blocked(x):
        return x.reshape(block_count, block_rows, head_count, head_width)

    def blocked_stat(x):
        return x.reshape(head_count, block_count, block_rows).transpose(1, 0, 2)

    def near_step(carry, pieces):
        query_b, dout_b, lse_b, delta_b = pieces
        grad_q, grad_k, grad_v = grads_core(query_b, dout_b, lse_b, delta_b, keys, values, scaling)
        return ((carry[0] + grad_k, carry[1] + grad_v), grad_q)

    zero_rows = jnp.zeros(queries.shape, jnp.float32)
    (near_k, near_v), near_q = lax.scan(
        near_step,
        (zero_rows, zero_rows),
        (blocked(queries), blocked(grad_out), blocked_stat(fine_lse), blocked_stat(delta_fine)),
    )
    near_q = near_q.reshape(row_count, head_count, head_width)

    def cubed(x):
        return x.reshape(cube_count, cube_len, head_count, head_width)

    def flatten(x):
        return x.reshape(row_count, head_count, head_width)

    query_cubes = cubed(queries)
    dout_cubes = cubed(grad_out)
    key_cubes = cubed(keys)
    value_cubes = cubed(values)
    pooled_keys = jnp.mean(key_cubes, axis=1, dtype=jnp.float32).astype(jnp.bfloat16)
    pooled_values = jnp.mean(value_cubes, axis=1, dtype=jnp.float32).astype(jnp.bfloat16)
    all_keys, all_values = (
        lax.all_gather(pooled_keys, "seq", axis=0, tiled=True),
        lax.all_gather(pooled_values, "seq", axis=0, tiled=True),
    )
    coarse_q, coarse_k, coarse_v = grads_core(
        queries, grad_out, coarse_lse, delta_coarse, all_keys, all_values, scaling
    )
    total_k, total_v = lax.psum((coarse_k, coarse_v), "seq")
    first_cube = lax.axis_index("seq") * cube_count
    own_k = lax.dynamic_slice_in_dim(total_k, first_cube, cube_count, 0)
    own_v = lax.dynamic_slice_in_dim(total_v, first_cube, cube_count, 0)
    targets = select.reshape(-1)
    dest = targets // cube_count
    local_cube = targets % cube_count
    task_index = jnp.arange(task_total, dtype=jnp.int32)
    earlier = (dest[None, :] == dest[:, None]) & (task_index[None, :] < task_index[:, None])
    slot_of_task = dest * slot_cap + jnp.sum(earlier.astype(jnp.int32), axis=1)
    matches = slot_of_task[None, :] == jnp.arange(slot_total, dtype=jnp.int32)[:, None]
    occupied = jnp.any(matches, axis=1)
    task_of_slot = jnp.sum(jnp.where(matches, task_index[None, :], 0), axis=1)
    cube_of_slot = jnp.where(
        occupied, jnp.sum(jnp.where(matches, local_cube[None, :], 0), axis=1), -1
    )
    lse_cubes = fine_lse.reshape(head_count, cube_count, cube_len).transpose(1, 0, 2)
    delta_cubes = delta_fine.reshape(head_count, cube_count, cube_len).transpose(1, 0, 2)
    cube_ids = jnp.arange(cube_count, dtype=jnp.int32)

    def to_slots(picked):
        mask = occupied.reshape((slot_total,) + (1,) * (picked.ndim - 1))
        kept = jnp.where(mask, picked, jnp.zeros_like(picked))
        return kept.reshape((seq_size, slot_cap) + picked.shape[1:])

    asked = lax.all_to_all(
        cube_of_slot.reshape(seq_size, slot_cap), "seq", split_axis=0, concat_axis=0, tiled=True
    ).reshape(-1)
    safe_ids = jnp.clip(asked, 0, cube_count - 1)
    slot_shape = (seq_size, slot_cap, cube_len, head_count, head_width)
    got_k, got_v = (
        lax.all_to_all(
            key_cubes[safe_ids].reshape(slot_shape), "seq", split_axis=0, concat_axis=0, tiled=True
        ),
        lax.all_to_all(
            value_cubes[safe_ids].reshape(slot_shape),
            "seq",
            split_axis=0,
            concat_axis=0,
            tiled=True,
        ),
    )
    got_k = got_k.reshape(slot_total, cube_len, head_count, head_width)
    got_v = got_v.reshape(slot_total, cube_len, head_count, head_width)
    query_of_task = task_index // far_count
    task_q, task_k, task_v = grads_core(
        query_cubes[query_of_task],
        dout_cubes[query_of_task],
        lse_cubes[query_of_task],
        delta_cubes[query_of_task],
        got_k[slot_of_task],
        got_v[slot_of_task],
        scaling,
    )
    rounded_q = lax.optimization_barrier(task_q.astype(jnp.bfloat16)).astype(jnp.float32)
    far_q = flatten(
        rounded_q.reshape(cube_count, far_count, cube_len, head_count, head_width).sum(axis=1)
    )
    back_k = to_slots(task_k.astype(jnp.bfloat16)[task_of_slot])
    back_v = to_slots(task_v.astype(jnp.bfloat16)[task_of_slot])
    part_k, part_v = (
        lax.all_to_all(back_k, "seq", split_axis=0, concat_axis=0, tiled=True),
        lax.all_to_all(back_v, "seq", split_axis=0, concat_axis=0, tiled=True),
    )
    slot_k = part_k.reshape(slot_total, cube_len, head_count, head_width)
    slot_v = part_v.reshape(slot_total, cube_len, head_count, head_width)
    pick_owned = (asked[:, None] == cube_ids[None, :]).astype(jnp.bfloat16)
    far_k = flatten(
        jnp.einsum("sc,sqhe->cqhe", pick_owned, slot_k, preferred_element_type=jnp.float32)
    )
    far_v = flatten(
        jnp.einsum("sc,sqhe->cqhe", pick_owned, slot_v, preferred_element_type=jnp.float32)
    )
    cube_shape = (cube_count, cube_len, head_count, head_width)
    spread_k = flatten(jnp.broadcast_to((own_k / cube_len)[:, None], cube_shape))
    spread_v = flatten(jnp.broadcast_to((own_v / cube_len)[:, None], cube_shape))
    grad_queries = (near_q + far_q + coarse_q).astype(jnp.bfloat16)
    grad_keys = (near_k + far_k + spread_k).astype(jnp.bfloat16)
    grad_values = (near_v + far_v + spread_v).astype(jnp.bfloat16)
    return (grad_queries, grad_keys, grad_values, own_k, own_v)


def solution(mesh):
    return jax.shard_map(
        shards,
        mesh=mesh,
        in_specs=(
            P(("groups", "seq"), ("head", "pair"), None),
            P(("groups", "seq"), ("head", "pair"), None),
            P(("groups", "seq"), ("head", "pair"), None),
            P(("groups", "seq"), ("head", "pair"), None),
            P(("groups", "seq"), ("head", "pair"), None),
            P(("groups", "seq"), ("head", "pair"), None),
            P(("head", "pair"), ("groups", "seq")),
            P(("head", "pair"), ("groups", "seq")),
            P(("groups", "seq"), None),
        ),
        out_specs=(
            P(("groups", "seq"), ("head", "pair"), None),
            P(("groups", "seq"), ("head", "pair"), None),
            P(("groups", "seq"), ("head", "pair"), None),
            P(("groups", "seq"), ("head", "pair"), None),
            P(("groups", "seq"), ("head", "pair"), None),
        ),
        check_vma=False,
    )
```

profile of v0, /device:TPU:0, one launch (start us, length us, event | category | flops | bytes accessed | tf_op | source)
XLA Modules:
  0.0 763.5 jit_solution(421882429742673855)
XLA Ops:
  9.0 11.7 %all_to_all.26 = s32[4,1,8]{2,1,0:T(1,128)S(1)} all-to-all(s32[4,1,8]{2,1,0:T(1,128)S(1)} %bitcast.206), channel_id=1, replica_groups=mesh['groups'=2,'seq'=4,'head'=2,'pair'=2] {'seq'}, dimensions={0} | all-to-all | bytes 256 | tf_op jit(solution)/shard_map/all_to_all | solution.py:108
  27.8 5.3 all-to-all-start.1
  36.7 111.0 %all-to-all-done.1 = bf16[4,8,64,10,128]{4,2,3,1,0:T(8,128)(2,1)} async-done(((bf16[4,8,64,10,128]{4,2,3,1,0:T(8,128)(2,1)}), bf16[4,8,64,10,128]{4,2,3,1,0:T(8,128)(2,1)}, u32[]{:S(2)}, u32[]{:S(2)}) %all-to-all-start.1) | async-done | bytes 5242912 | tf_op jit(solution)/shard_map/all_to_all | solution.py:114
  147.7 5.5 all-to-all-start.2
  170.1 98.2 %all-to-all-done.2 = bf16[4,8,64,10,128]{4,2,3,1,0:T(8,128)(2,1)} async-done(((bf16[4,8,64,10,128]{4,2,3,1,0:T(8,128)(2,1)}), bf16[4,8,64,10,128]{4,2,3,1,0:T(8,128)(2,1)}, u32[]{:S(2)}, u32[]{:S(2)}) %all-to-all-start.2) | async-done | bytes 5242912 | tf_op jit(solution)/shard_map/all_to_all | solution.py:117
  296.9 8.7 %broadcast_select_fusion = (bf16[4,8,64,10,128]{4,2,3,1,0:T(8,128)(2,1)}, bf16[4,8,64,10,128]{4,2,3,1,0:T(8,128)(2,1)}) fusion(bf16[4,8,64,10,128]{4,2,3,1,0:T(8,128)(2,1)} %bitcast.192, pred[4,8]{1,0:T(4,128)(4,1)S(1)} %broadcast_in_dim.52, bf16[4,8,64,10,128]{4,2,3,1,0:T(8,128)(2,1)} %bitcast.193), kind=kLoop, calls=%fused_computation.61 | loop fusion | flops 5242880 | bytes 20971552 | tf_op jit(solution)/shard_map/jit(_where)/select_n | solution.py:105
  305.6 5.3 all-to-all-start.3
  311.9 120.8 %all_gather.6 = bf16[64,10,128]{2,0,1:T(8,128)(2,1)S(1)} all-gather(bf16[16,10,128]{2,0,1:T(8,128)(2,1)S(1)} %multiply_convert_fusion.6), channel_id=1, replica_groups=mesh['groups'=2,'seq'=4,'head'=2,'pair'=2] {'seq'}, dimensions={0}, use_global_device_ids=true | all-gather | bytes 204800 | tf_op jit(solution)/shard_map/all_gather | solution.py:77
  435.4 13.5 %all_gather.7 = bf16[64,10,128]{2,0,1:T(8,128)(2,1)S(1)} all-gather(bf16[16,10,128]{2,0,1:T(8,128)(2,1)S(1)} %multiply_convert_fusion.5), channel_id=1, replica_groups=mesh['groups'=2,'seq'=4,'head'=2,'pair'=2] {'seq'}, dimensions={0}, use_global_device_ids=true | all-gather | bytes 204800 | tf_op jit(solution)/shard_map/all_gather | solution.py:78
  459.0 213.6 %while.15 = (s32[]{:T(128)}, f32[1024,10,128]{0,2,1:T(8,128)}, f32[1024,10,128]{0,2,1:T(8,128)}, f32[2,512,10,128]{1,0,3,2:T(2,128)}, bf16[2,512,10,128]{3,1,0,2...) while((s32[]{:T(128)}, f32[1024,10,128]{0,2,1:T(8,128)}, ...), condition=%wide.region_1.2_spmd.clone, body=%wide.region_0.1_spmd.clone.sunk | while | flops 6760038400 | bytes 152281280 | solution.py:57
  459.0 9.9 %fusion.110 = f32[10,512,1024]{2,1,0:T(8,128)} fusion(bf16[1024,10,128]{2,0,1:T(8,128)(2,1)S(1)} %get-tuple-element.296, bf16[2,512,10,128]{3,1,0,2:T(8,128)(2,1)} %get-tuple-element.295, s32[]{:T(128)S(6)} %copy.158), kind=kOutput, calls=%fused_computation.22.clone.1 | convolution fusion | flops 1342177280 | bytes 24903684 | tf_op jit(solution)/shard_map/while/body/eval_jaxpr/...qhe,...khe->...hqk/dot_general | solution.py:8
  469.0 13.1 %multiply_convert_fusion.8 = bf16[10,512,1024]{2,1,0:T(8,128)(2,1)} fusion(f32[10,512,1024]{2,1,0:T(8,128)} %fusion.110, f32[10,512]{1,0:T(8,128)S(1)} %bitcast.201, f32[10,512]{1,0:T(8,128)S(1)} %bitcast.199, bf16[1024,10,128]{2,0,1:T(8,128)(2,1)} %get-tuple-element.299, bf16[2,512,10,128]{3,1,0,2:T(8,128)(2,1)} %get-tuple-element.298, s32[]{:T(128)S(6)} %copy.158), kind=kOutput, calls=%fused_computation.10.clone.1 | convolution fusion | flops 1368391680 | bytes 35430404 | tf_op jit(solution)/shard_map/while/body/eval_jaxpr/...qhe,...khe->...hqk/dot_general | solution.py:13
  482.1 9.0 %bitcast_add_fusion.10 = f32[1024,10,128]{0,2,1:T(8,128)} fusion(f32[1024,10,128]{0,2,1:T(8,128)} %get-tuple-element.280, pred[]{:T(512)S(6)} %compare.24, bf16[10,512,1024]{2,1,0:T(8,128)(2,1)} %multiply_convert_fusion.8, bf16[2,512,10,128]{3,1,0,2:T(8,128)(2,1)} %get-tuple-element.295, s32[]{:T(128)S(6)} %copy.158), kind=kOutput, calls=%fused_computation.17.clone.1 | convolution fusion | flops 1346109440 | bytes 22282244 | tf_op jit(solution)/shard_map/while/body/eval_jaxpr/...hqk,...qhe->...khe/dot_general | solution.py:20
  491.1 10.7 %bitcast_add_fusion.11 = f32[1024,10,128]{0,2,1:T(8,128)} fusion(f32[1024,10,128]{0,2,1:T(8,128)} %get-tuple-element.281, pred[]{:T(512)S(6)} %compare.24, f32[10,512,1024]{2,1,0:T(8,128)} %fusion.110, f32[10,512]{1,0:T(8,128)S(1)} %bitcast.200, bf16[2,512,10,128]{3,1,0,2:T(8,128)(2,1)S(1)} %copy-done.3, s32[]{:T(128)S(6)} %copy.158), kind=kOutput, calls=%fused_computation.16.clone.1 | convolution fusion | flops 1360527360 | bytes 32800772 | tf_op jit(solution)/shard_map/while/body/eval_jaxpr/...hqk,...qhe->...khe/dot_general | solution.py:23
  501.8 8.4 %multiply_bitcast_fusion.2 = f32[1,512,10,128]{3,1,2,0:T(8,128)} fusion(bf16[10,512,1024]{2,1,0:T(8,128)(2,1)} %multiply_convert_fusion.8, bf16[1024,10,128]{2,0,1:T(8,128)(2,1)S(1)} %get-tuple-element.296), kind=kOutput, calls=%fused_computation.18.clone.1 | convolution fusion | flops 1342832640 | bytes 15728640 | tf_op jit(solution)/shard_map/while/body/eval_jaxpr/...hqk,...khe->...qhe/dot_general | solution.py:17
  510.2 6.4 copy.152
  516.6 47.4 %dynamic_update_slice.6 = f32[2,512,10,128]{1,0,3,2:T(2,128)} dynamic-update-slice(f32[2,512,10,128]{1,0,3,2:T(2,128)} %get-tuple-element.282, f32[1,512,10,128]{1,0,3,2:T(1,128)} %copy.152, s32[]{:T(128)S(6)} %copy.158, s32[]{:T(128)} %constant.77.clone.1..sunk, s32[]{:T(128)} %constant.77.clone.1..sunk, s32[]{:T(128)} %constant.77.clone.1..sunk) | dynamic-update-slice | bytes 5242884 | tf_op jit(solution)/shard_map/while/body/jit(dynamic_update_index_in_dim)/dynamic_update_slice | solution.py:57
  564.0 9.9 %fusion.110 = f32[10,512,1024]{2,1,0:T(8,128)} fusion(bf16[1024,10,128]{2,0,1:T(8,128)(2,1)S(1)} %get-tuple-element.296, bf16[2,512,10,128]{3,1,0,2:T(8,128)(2,1)} %get-tuple-element.295, s32[]{:T(128)S(6)} %copy.158), kind=kOutput, calls=%fused_computation.22.clone.1 | convolution fusion | flops 1342177280 | bytes 24903684 | tf_op jit(solution)/shard_map/while/body/eval_jaxpr/...qhe,...khe->...hqk/dot_general | solution.py:8
  573.9 13.0 %multiply_convert_fusion.8 = bf16[10,512,1024]{2,1,0:T(8,128)(2,1)} fusion(f32[10,512,1024]{2,1,0:T(8,128)} %fusion.110, f32[10,512]{1,0:T(8,128)S(1)} %bitcast.201, f32[10,512]{1,0:T(8,128)S(1)} %bitcast.199, bf16[1024,10,128]{2,0,1:T(8,128)(2,1)} %get-tuple-element.299, bf16[2,512,10,128]{3,1,0,2:T(8,128)(2,1)} %get-tuple-element.298, s32[]{:T(128)S(6)} %copy.158), kind=kOutput, calls=%fused_computation.10.clone.1 | convolution fusion | flops 1368391680 | bytes 35430404 | tf_op jit(solution)/shard_map/while/body/eval_jaxpr/...qhe,...khe->...hqk/dot_general | solution.py:13
  586.9 10.5 %bitcast_add_fusion.10 = f32[1024,10,128]{0,2,1:T(8,128)} fusion(f32[1024,10,128]{0,2,1:T(8,128)} %get-tuple-element.280, pred[]{:T(512)S(6)} %compare.24, bf16[10,512,1024]{2,1,0:T(8,128)(2,1)} %multiply_convert_fusion.8, bf16[2,512,10,128]{3,1,0,2:T(8,128)(2,1)} %get-tuple-element.295, s32[]{:T(128)S(6)} %copy.158), kind=kOutput, calls=%fused_computation.17.clone.1 | convolution fusion | flops 1346109440 | bytes 22282244 | tf_op jit(solution)/shard_map/while/body/eval_jaxpr/...hqk,...qhe->...khe/dot_general | solution.py:20
  597.4 13.1 %bitcast_add_fusion.11 = f32[1024,10,128]{0,2,1:T(8,128)} fusion(f32[1024,10,128]{0,2,1:T(8,128)} %get-tuple-element.281, pred[]{:T(512)S(6)} %compare.24, f32[10,512,1024]{2,1,0:T(8,128)} %fusion.110, f32[10,512]{1,0:T(8,128)S(1)} %bitcast.200, bf16[2,512,10,128]{3,1,0,2:T(8,128)(2,1)S(1)} %copy-done.3, s32[]{:T(128)S(6)} %copy.158), kind=kOutput, calls=%fused_computation.16.clone.1 | convolution fusion | flops 1360527360 | bytes 32800772 | tf_op jit(solution)/shard_map/while/body/eval_jaxpr/...hqk,...qhe->...khe/dot_general | solution.py:23
  610.5 8.3 %multiply_bitcast_fusion.2 = f32[1,512,10,128]{3,1,2,0:T(8,128)} fusion(bf16[10,512,1024]{2,1,0:T(8,128)(2,1)} %multiply_convert_fusion.8, bf16[1024,10,128]{2,0,1:T(8,128)(2,1)S(1)} %get-tuple-element.296), kind=kOutput, calls=%fused_computation.18.clone.1 | convolution fusion | flops 1342832640 | bytes 15728640 | tf_op jit(solution)/shard_map/while/body/eval_jaxpr/...hqk,...khe->...qhe/dot_general | solution.py:17
  618.8 6.4 copy.152
  625.2 47.4 %dynamic_update_slice.6 = f32[2,512,10,128]{1,0,3,2:T(2,128)} dynamic-update-slice(f32[2,512,10,128]{1,0,3,2:T(2,128)} %get-tuple-element.282, f32[1,512,10,128]{1,0,3,2:T(1,128)} %copy.152, s32[]{:T(128)S(6)} %copy.158, s32[]{:T(128)} %constant.77.clone.1..sunk, s32[]{:T(128)} %constant.77.clone.1..sunk, s32[]{:T(128)} %constant.77.clone.1..sunk) | dynamic-update-slice | bytes 5242884 | tf_op jit(solution)/shard_map/while/body/jit(dynamic_update_index_in_dim)/dynamic_update_slice | solution.py:57
  672.6 8.3 %reshape.237 = f32[1024,10,128]{0,2,1:T(8,128)} reshape(f32[2,512,10,128]{1,0,3,2:T(2,128)} %get-tuple-element.59) | data formatting | bytes 10485760 | tf_op jit(solution)/shard_map/reshape | solution.py:62
  680.9 5.9 copy.98
  686.8 6.1 copy.102
  700.2 6.0 copy.94
  706.2 6.5 fusion.29
  717.1 12.9 %fusion.27 = f32[16,64,10,128]{3,0,2,1:T(8,128)S(1)} fusion(bf16[4,8,64,10,128]{4,2,3,1,0:T(8,128)(2,1)} %all-to-all-done.3, s32[32]{0:T(128)S(1)} %eq.54), kind=kOutput, calls=%fused_computation.49 | convolution fusion | flops 83886592 | bytes 10485888 | tf_op jit(solution)/shard_map/sc,sqhe->cqhe/dot_general | solution.py:151
  730.0 5.5 copy.97
  735.5 13.3 %fusion.24 = f32[16,64,10,128]{3,0,2,1:T(8,128)S(1)} fusion(bf16[4,8,64,10,128]{4,2,3,1,0:T(8,128)(2,1)} %all-to-all-done.4, s32[32]{0:T(128)S(1)} %eq.54), kind=kOutput, calls=%fused_computation.44 | convolution fusion | flops 83886592 | bytes 10485888 | tf_op jit(solution)/shard_map/sc,sqhe->cqhe/dot_general | solution.py:154
  (125 shorter events, 90.5 us)
Async XLA Ops:
  27.8 5.4 copy-start.4
  27.8 119.9 %all-to-all-start.1 = ((bf16[4,8,64,10,128]{4,2,3,1,0:T(8,128)(2,1)}), bf16[4,8,64,10,128]{4,2,3,1,0:T(8,128)(2,1)}, u32[]{:S(2)}, u32[]{:S(2)}) async-start(bf16[4,8,64,10,128]{4,2,3,1,0:T(8,128)(2,1)} %bitcast.191), calls=%async_computation.1 | async-start | bytes 10485760 | tf_op jit(solution)/shard_map/all_to_all | solution.py:114
  147.7 5.6 copy-start.1
  147.7 120.7 %all-to-all-start.2 = ((bf16[4,8,64,10,128]{4,2,3,1,0:T(8,128)(2,1)}), bf16[4,8,64,10,128]{4,2,3,1,0:T(8,128)(2,1)}, u32[]{:S(2)}, u32[]{:S(2)}) async-start(bf16[4,8,64,10,128]{4,2,3,1,0:T(8,128)(2,1)} %bitcast.190), calls=%async_computation.2 | async-start | bytes 10485760 | tf_op jit(solution)/shard_map/all_to_all | solution.py:117
  158.6 4.8 copy-start.18
  162.9 3.6 copy-start.20
  170.1 103.1 %copy-start.6 = (bf16[16,64,10,128]{3,1,2,0:T(8,128)(2,1)}, bf16[16,64,10,128]{3,1,2,0:T(8,128)(2,1)S(1)}, u32[]{:S(2)}) copy-start(bf16[16,64,10,128]{3,1,2,0:T(8,128)(2,1)S(1)} %gather_fusion.1) | copy-start | bytes 7864324
  273.2 3.4 copy-start.9
  276.6 3.8 copy-start.12
  280.4 5.0 copy-start.8
  283.9 1.5 copy-start.10
  305.6 5.4 copy-start
  305.6 148.3 %all-to-all-start.3 = ((bf16[4,8,64,10,128]{4,2,3,1,0:T(8,128)(2,1)}), bf16[4,8,64,10,128]{4,2,3,1,0:T(8,128)(2,1)}, u32[]{:S(2)}, u32[]{:S(2)}) async-start(bf16[4,8,64,10,128]{4,2,3,1,0:T(8,128)(2,1)} %get-tuple-element.195), calls=%async_computation.3 | async-start | bytes 10485760 | tf_op jit(solution)/shard_map/all_to_all | solution.py:144
  310.9 139.0 %copy-start.17 = (f32[10,1024]{1,0:T(8,128)S(1)}, f32[10,1024]{1,0:T(8,128)}, u32[]{:S(2)}) copy-start(f32[10,1024]{1,0:T(8,128)} %param.18) | copy-start | bytes 122884
  311.0 382.1 %all-reduce.3.cloned.1.call-start = ((), (), s32[]{:S(2)}) async-start(), calls=%async_computation.5 | async-start | bytes 1310720 | tf_op jit(solution)/shard_map/psum | solution.py:83
  311.0 137.9 %copy-start.5 = (bf16[1024,10,128]{2,0,1:T(8,128)(2,1)S(1)}, bf16[1024,10,128]{2,0,1:T(8,128)(2,1)}, u32[]{:S(2)}) copy-start(bf16[1024,10,128]{2,0,1:T(8,128)(2,1)} %param.11) | copy-start | bytes 7864324
  311.0 138.9 %copy-start.2 = (bf16[1024,10,128]{2,0,1:T(8,128)(2,1)S(1)}, bf16[1024,10,128]{2,0,1:T(8,128)(2,1)}, u32[]{:S(2)}) copy-start(bf16[1024,10,128]{2,0,1:T(8,128)(2,1)} %param.14) | copy-start | bytes 7864324
  432.7 17.2 %copy-start.15 = (bf16[64,10,128]{2,0,1:T(8,128)(2,1)}, bf16[64,10,128]{2,0,1:T(8,128)(2,1)S(1)}, u32[]{:S(2)}) copy-start(bf16[64,10,128]{2,0,1:T(8,128)(2,1)S(1)} %all_gather.6) | copy-start | bytes 491524
  451.0 1.4 copy-start.13
  453.9 281.6 %all-to-all-start.4 = ((bf16[4,8,64,10,128]{4,2,3,1,0:T(8,128)(2,1)}), bf16[4,8,64,10,128]{4,2,3,1,0:T(8,128)(2,1)}, u32[]{:S(2)}, u32[]{:S(2)}) async-start(bf16[4,8,64,10,128]{4,2,3,1,0:T(8,128)(2,1)} %get-tuple-element.194), calls=%async_computation.4 | async-start | bytes 10485760 | tf_op jit(solution)/shard_map/all_to_all | solution.py:145
  482.1 9.0 %copy-start.3 = (bf16[2,512,10,128]{3,1,0,2:T(8,128)(2,1)S(1)}, bf16[2,512,10,128]{3,1,0,2:T(8,128)(2,1)}, u32[]{:S(2)}) copy-start(bf16[2,512,10,128]{3,1,0,2:T(8,128)(2,1)} %get-tuple-element.298) | copy-start | bytes 7864324 | tf_op jit(solution)/shard_map/while
  586.9 10.5 %copy-start.3 = (bf16[2,512,10,128]{3,1,0,2:T(8,128)(2,1)S(1)}, bf16[2,512,10,128]{3,1,0,2:T(8,128)(2,1)}, u32[]{:S(2)}) copy-start(bf16[2,512,10,128]{3,1,0,2:T(8,128)(2,1)} %get-tuple-element.298) | copy-start | bytes 7864324 | tf_op jit(solution)/shard_map/while
  686.8 6.1 copy-start.19
  686.8 7.8 %copy-start.7 = (bf16[16,64,10,128]{3,1,2,0:T(8,128)(2,1)S(1)}, bf16[16,64,10,128]{3,1,2,0:T(8,128)(2,1)}, u32[]{:S(2)}) copy-start(bf16[16,64,10,128]{3,1,2,0:T(8,128)(2,1)} %copy-done.6) | copy-start | bytes 7864324
  700.2 6.0 copy-start.14
  700.2 6.0 copy-start.16
  735.5 16.4 %slice-start = ((s8[5242880]{0:T(1024)(128)(4,1)}), s8[4194304]{0:T(1024)(128)(4,1)S(1)}, s32[]{:S(2)}) async-start(s8[5242880]{0:T(1024)(128)(4,1)} %bitcast.194), calls=%async_computation.6 | async-start | bytes 8388608
  748.8 3.1 slice-start.1
  748.8 3.1 copy-start.11
  748.8 5.3 slice-start.2
  751.9 2.2 slice-start.3
Sparse Core Ops, SparseCore 0:
  453.9 79.4 all-reduce.2
where the time goes:
time: 774 us; the launch traced here: 764 us
  waiting for transfers between devices  209 us (27%)
  local copies, waits for them, and re-layouts  186 us (24%)
  matrix products  159 us (21%)
  blocking collectives  146 us (19%)
  other arithmetic  26.5 us (3%)
  starting transfers between devices  21.3 us (3%)
  between operations  14.9 us (2%)
    all_gather x1, blocking collectives, shards(): lax.all_gather(pooled_keys, 'seq', axis=0, tiled=True)  121 us
    all_to_all x1, waiting for transfers between devices, shards(): lax.all_to_all(key_cubes[safe_ids].reshape(slot_shape), 'seq', split_axis...  111 us
    dynamic_update_slice x4, local copies, waits for them, and re-layouts, shards(): lax.scan(near_step, (zero_rows, zero_rows), (blocked(queries), blocked(gr...  108 us
    all_to_all x1, waiting for transfers between devices, shards(): lax.all_to_all(value_cubes[safe_ids].reshape(slot_shape), 'seq', split_ax...  98.2 us
    dot_general x4, matrix products, grads_core(): jnp.einsum('...qhe,...khe->...hqk', dout_x, value_x, preferred_element_ty...  30.6 us
    dot_general x4, matrix products, grads_core(): jnp.einsum('...hqk,...qhe->...khe', probs_low, dout_x, preferred_element_...  29 us
    dot_general x4, matrix products, grads_core(): jnp.einsum('...hqk,...khe->...qhe', dscores, key_x, preferred_element_typ...  25.7 us
    dot_general x4, matrix products, grads_core(): jnp.einsum('...qhe,...khe->...hqk', query_x, key_x, preferred_element_typ...  24.2 us
  transfers between devices with their start and end apart: 5, of which 2 were waited for; matrix products, arithmetic and copies ran while one was open for 40% of the time, Pallas kernels for 0%

commit v1 on v0

v1 whole, which is shorter than its diff:
```python
import functools

import jax
import jax.numpy as jnp
from jax import lax
from jax.experimental import pallas as pl
from jax.experimental.pallas import tpu as pltpu
from jax.sharding import PartitionSpec as P

F32 = jnp.float32
BF16 = jnp.bfloat16
VMEM_BYTES = 48 * 1024 * 1024
OFF_LSE = 1e30


def dot_nt(a, b):
    return lax.dot_general(a, b, (((1,), (1,)), ((), ())), preferred_element_type=F32)


def dot_nn(a, b):
    return lax.dot_general(a, b, (((1,), (0,)), ((), ())), preferred_element_type=F32)


def dot_tn(a, b):
    return lax.dot_general(a, b, (((0,), (0,)), ((), ())), preferred_element_type=F32)


def block_rule(q, do, lse, delta, k, v, scaling):
    probs = jnp.exp(dot_nt(k, q) * scaling - lse)
    dscores = (probs * (dot_nt(v, do) - delta)).astype(BF16)
    return probs.astype(BF16), dscores


def params(**more):
    return pltpu.CompilerParams(vmem_limit_bytes=VMEM_BYTES, **more)


def pack_kernel(splits, task_ref, q_ref, do_ref, *outs):
    for part, ref in ((0, q_ref), (1, do_ref)):
        flipped = jnp.swapaxes(ref[...].astype(F32), 0, 1).astype(BF16)
        for (low, high), out in zip(splits, outs):
            out[0, part] = flipped[low:high]


def pack(queries, grad_out, task_of_slot, cube_len, far_count, splits):
    _, heads, width = queries.shape
    slots = task_of_slot.shape[0]
    source = pl.BlockSpec((cube_len, heads, width), lambda s, t: (t[s] // far_count, 0, 0))
    sizes = [(2, high - low, cube_len, width) for low, high in splits]
    return pl.pallas_call(
        functools.partial(pack_kernel, splits),
        grid_spec=pltpu.PrefetchScalarGridSpec(
            num_scalar_prefetch=1,
            grid=(slots,),
            in_specs=[source, source],
            out_specs=[pl.BlockSpec((1,) + size, lambda s, t: (s, 0, 0, 0, 0)) for size in sizes],
        ),
        out_shape=[jax.ShapeDtypeStruct((slots,) + size, BF16) for size in sizes],
        compiler_params=params(),
    )(task_of_slot, queries, grad_out)


def near_kernel(
    scaling, chunk, q_ref, do_ref, k_ref, v_ref, pk_ref, pv_ref, stat_ref,
    dq_ref, dk_ref, dv_ref, ck_ref, cv_ref,
):
    rows = q_ref.shape[1]
    k, v, pk, pv = k_ref[0], v_ref[0], pk_ref[0], pv_ref[0]
    for start in range(0, rows, chunk):
        at = slice(start, start + chunk)
        q, do = q_ref[0, at, :], do_ref[0, at, :]
        fine = block_rule(q, do, stat_ref[0, 0:1, at], stat_ref[0, 1:2, at], k, v, scaling)
        coarse = block_rule(q, do, stat_ref[0, 2:3, at], stat_ref[0, 3:4, at], pk, pv, scaling)
        dq_ref[0, at, :] = scaling * (dot_tn(fine[1], k) + dot_tn(coarse[1], pk))
        for (probs, dscores), key_out, value_out in (
            (fine, dk_ref, dv_ref),
            (coarse, ck_ref, cv_ref),
        ):
            grad_k = scaling * dot_nn(dscores, q)
            grad_v = dot_nn(probs, do)
            if start == 0:
                key_out[0] = grad_k
                value_out[0] = grad_v
            else:
                key_out[0] += grad_k
                value_out[0] += grad_v


def near(q, do, k, v, pooled_k, pooled_v, stats, scaling):
    heads, rows, width = q.shape
    pooled = pooled_k.shape[1]
    token = pl.BlockSpec((1, rows, width), lambda h: (h, 0, 0))
    cube = pl.BlockSpec((1, pooled, width), lambda h: (h, 0, 0))
    token_out = jax.ShapeDtypeStruct((heads, rows, width), F32)
    cube_out = jax.ShapeDtypeStruct((heads, pooled, width), F32)
    return pl.pallas_call(
        functools.partial(near_kernel, scaling, min(256, rows)),
        grid=(heads,),
        in_specs=[token] * 4 + [cube] * 2 + [pl.BlockSpec((1, 4, rows), lambda h: (h, 0, 0))],
        out_specs=[token] * 3 + [cube] * 2,
        out_shape=[token_out] * 3 + [cube_out] * 2,
        compiler_params=params(),
        cost_estimate=pl.CostEstimate(
            flops=20 * heads * rows * (rows + pooled) * width,
            bytes_accessed=heads * rows * width * 20,
            transcendentals=heads * rows * (rows + pooled),
        ),
    )(q, do, k, v, pooled_k, pooled_v, stats)


def far_kernel(
    scaling, cap, asked_ref, got_ref, stat_ref, k_ref, v_ref, nk_ref, nv_ref, ok_ref, ov_ref,
    dq_ref, gk_ref, gv_ref, acc_k, acc_v,
):
    cubes, width = ok_ref.shape[1:]
    cube_len = k_ref.shape[1] // cubes
    for cube in range(cubes):
        at = slice(cube * cube_len, (cube + 1) * cube_len)
        acc_k[at, :] = nk_ref[0, at, :] + ok_ref[0, cube : cube + 1, :] * (1.0 / cube_len)
        acc_v[at, :] = nv_ref[0, at, :] + ov_ref[0, cube : cube + 1, :] * (1.0 / cube_len)
    me = lax.axis_index("seq")

    def from_source(source, carry):
        @pl.when(source != me)
        def _():
            pending = []
            for slot in range(cap):
                index = source * cap + slot
                first = pl.multiple_of(
                    jnp.maximum(asked_ref[index], 0) * cube_len, cube_len
                )
                at = pl.ds(first, cube_len)
                k, v = k_ref[0, at, :], v_ref[0, at, :]
                q, do = got_ref[index, 0, 0], got_ref[index, 1, 0]
                stat = stat_ref[0, pl.ds(index, 1), :]
                probs, dscores = block_rule(
                    q, do, stat[:, :cube_len], stat[:, cube_len:], k, v, scaling
                )
                dq_ref[index, 0] = (scaling * dot_tn(dscores, k)).astype(BF16)
                task_k = (scaling * dot_nn(dscores, q)).astype(BF16)
                task_v = dot_nn(probs, do).astype(BF16)
                pending.append((at, task_k, task_v))
            for at, task_k, task_v in pending:
                acc_k[at, :] += task_k.astype(F32)
                acc_v[at, :] += task_v.astype(F32)

        return carry

    lax.fori_loop(0, dq_ref.shape[0] // cap, from_source, 0)
    gk_ref[0] = acc_k[...].astype(BF16)
    gv_ref[0] = acc_v[...].astype(BF16)


def far(asked, got, stats, k, v, near_k, near_v, own_k, own_v, low, cap, scaling):
    slots, _, heads, cube_len, width = got.shape
    rows = k.shape[1]
    cubes = own_k.shape[1]
    token = pl.BlockSpec((1, rows, width), lambda h, a: (h + low, 0, 0))
    cube = pl.BlockSpec((1, cubes, width), lambda h, a: (h + low, 0, 0))
    out = pl.BlockSpec((1, rows, width), lambda h, a: (h, 0, 0))
    return pl.pallas_call(
        functools.partial(far_kernel, scaling, cap),
        grid_spec=pltpu.PrefetchScalarGridSpec(
            num_scalar_prefetch=1,
            grid=(heads,),
            in_specs=[
                pl.BlockSpec((slots, 2, 1, cube_len, width), lambda h, a: (0, 0, h, 0, 0)),
                pl.BlockSpec((1, slots, 2 * cube_len), lambda h, a: (h + low, 0, 0)),
                token, token, token, token, cube, cube,
            ],
            out_specs=[
                pl.BlockSpec((slots, 1, cube_len, width), lambda h, a: (0, h, 0, 0)),
                out,
                out,
            ],
            scratch_shapes=[pltpu.VMEM((rows, width), F32)] * 2,
        ),
        out_shape=[
            jax.ShapeDtypeStruct((slots, heads, cube_len, width), BF16),
            jax.ShapeDtypeStruct((heads, rows, width), BF16),
            jax.ShapeDtypeStruct((heads, rows, width), BF16),
        ],
        compiler_params=params(),
        cost_estimate=pl.CostEstimate(
            flops=100 * heads * slots * cube_len * cube_len * width,
            bytes_accessed=heads * rows * width * 30,
            transcendentals=heads * slots * cube_len * cube_len,
        ),
    )(asked, got, stats, k, v, near_k, near_v, own_k, own_v)


def join_kernel(splits, far_count, slot_ref, nq_ref, *refs):
    out = refs[-1]
    pieces = refs[:-1]
    total = []
    for part, (low, high) in enumerate(splits):
        piece = nq_ref[low:high]
        for far_at in range(far_count):
            piece = piece + pieces[part * far_count + far_at][0].astype(F32)
        total.append(piece)
    out[...] = jnp.swapaxes(jnp.concatenate(total, axis=0), 0, 1).astype(BF16)


def join(near_q, back, slot_of_task, cube_len, far_count, splits):
    heads, rows, width = near_q.shape
    specs, operands = [], []
    for (low, high), array in zip(splits, back):
        for far_at in range(far_count):
            specs.append(
                pl.BlockSpec(
                    (1, high - low, cube_len, width),
                    lambda c, s, far_at=far_at: (s[c * far_count + far_at], 0, 0, 0),
                )
            )
            operands.append(array)
    return pl.pallas_call(
        functools.partial(join_kernel, splits, far_count),
        grid_spec=pltpu.PrefetchScalarGridSpec(
            num_scalar_prefetch=1,
            grid=(rows // cube_len,),
            in_specs=[pl.BlockSpec((heads, cube_len, width), lambda c, s: (0, c, 0))] + specs,
            out_specs=pl.BlockSpec((cube_len, heads, width), lambda c, s: (c, 0, 0)),
        ),
        out_shape=jax.ShapeDtypeStruct((rows, heads, width), BF16),
        compiler_params=params(),
    )(slot_of_task, near_q, *operands)


def exchange(x):
    return lax.all_to_all(x, "seq", split_axis=0, concat_axis=0, tiled=True)


def shards(queries, keys, values, grad_out, fine_out, coarse_out, fine_lse, coarse_lse, select):
    rows, heads, width = queries.shape
    cubes, far_count = select.shape
    cube_len = rows // cubes
    scaling = width ** (-0.5)
    seq_size = lax.axis_size("seq")
    cap = max(2, min(cubes * far_count // 2, 3 * cubes * far_count // seq_size))
    slots = seq_size * cap
    tasks = cubes * far_count
    half = heads // 2
    splits = ((0, half), (half, heads))

    targets = select.reshape(-1)
    dest = targets // cubes
    local_cube = targets % cubes
    task_index = jnp.arange(tasks, dtype=jnp.int32)
    earlier = (dest[None, :] == dest[:, None]) & (task_index[None, :] < task_index[:, None])
    slot_of_task = dest * cap + jnp.sum(earlier.astype(jnp.int32), axis=1)
    matches = slot_of_task[None, :] == jnp.arange(slots, dtype=jnp.int32)[:, None]
    occupied = jnp.any(matches, axis=1)
    task_of_slot = jnp.sum(jnp.where(matches, task_index[None, :], 0), axis=1)
    cube_of_slot = jnp.where(
        occupied, jnp.sum(jnp.where(matches, local_cube[None, :], 0), axis=1), -1
    )

    sends = pack(queries, grad_out, task_of_slot, cube_len, far_count, splits)
    gots = [exchange(send.reshape((seq_size, cap) + send.shape[1:])) for send in sends]
    gots = [got.reshape((slots,) + got.shape[2:]) for got in gots]

    delta_fine = jnp.einsum("the,the->ht", grad_out, fine_out, preferred_element_type=F32)
    delta_coarse = jnp.einsum("the,the->ht", grad_out, coarse_out, preferred_element_type=F32)

    def task_stat(x):
        return x.reshape(heads, cubes, cube_len).transpose(1, 0, 2)[task_of_slot // far_count]

    slot_lse = jnp.where(occupied[:, None, None], task_stat(fine_lse), OFF_LSE)
    slot_stats = jnp.concatenate([slot_lse, task_stat(delta_fine)], axis=2)
    got_stats = exchange(slot_stats.reshape(seq_size, cap, heads, 2 * cube_len))
    got_stats = got_stats.reshape(slots, heads, 2 * cube_len).transpose(1, 0, 2)
    asked = exchange(cube_of_slot.reshape(seq_size, cap)).reshape(-1)

    def pooled(x):
        mean = jnp.mean(x.reshape(cubes, cube_len, heads, width), axis=1, dtype=F32)
        return mean.astype(BF16).transpose(1, 0, 2)

    all_pooled = lax.all_gather(
        jnp.concatenate([pooled(keys), pooled(values)], axis=0), "seq", axis=1, tiled=True
    )
    q, do, k, v = (x.transpose(1, 0, 2) for x in (queries, grad_out, keys, values))
    stats = jnp.stack([fine_lse, delta_fine, coarse_lse, delta_coarse], axis=1)
    near_q, near_k, near_v, coarse_k, coarse_v = near(
        q, do, k, v, all_pooled[:heads], all_pooled[heads:], stats, scaling
    )
    own = lax.psum_scatter(
        jnp.concatenate([coarse_k, coarse_v], axis=0), "seq", scatter_dimension=1, tiled=True
    )
    own_k, own_v = own[:heads], own[heads:]

    back, grads_k, grads_v = [], [], []
    for (low, high), got in zip(splits, gots):
        task_q, grad_k, grad_v = far(
            asked, got, got_stats, k, v, near_k, near_v, own_k, own_v, low, cap, scaling
        )
        returned = exchange(task_q.reshape((seq_size, cap) + task_q.shape[1:]))
        back.append(returned.reshape(task_q.shape))
        grads_k.append(grad_k)
        grads_v.append(grad_v)
    grad_queries = join(near_q, back, slot_of_task, cube_len, far_count, splits)
    grad_keys = jnp.concatenate(grads_k, axis=0).transpose(1, 0, 2)
    grad_values = jnp.concatenate(grads_v, axis=0).transpose(1, 0, 2)
    return (
        grad_queries,
        grad_keys,
        grad_values,
        own_k.transpose(1, 0, 2),
        own_v.transpose(1, 0, 2),
    )


def solution(mesh):
    token = P(("groups", "seq"), ("head", "pair"), None)
    stat = P(("head", "pair"), ("groups", "seq"))
    return jax.shard_map(
        shards,
        mesh=mesh,
        in_specs=(token,) * 6 + (stat, stat, P(("groups", "seq"), None)),
        out_specs=(token,) * 5,
        check_vma=False,
    )
```

time: 774 us -> 556 us (0.72); the launches traced: 764 us -> 554 us
  local copies, waits for them, and re-layouts: 186 us -> 24.7 us
  matrix products: 159 us -> 0 us
  Pallas kernels: 0 us -> 131 us
  waiting for transfers between devices: 209 us -> 100 us
  blocking collectives: 146 us -> 240 us
    dot_general x22 -> x0, matrix products: 159 us -> none  [the longest x4 30.6 us: grads_core(): jnp.einsum('...qhe,...khe->...hqk', dout_x, value_x, preferred_element_ty...]
    all_to_all x4 -> x5, waiting for transfers between devices: 209 us -> 77.9 us  [exchange(): return lax.all_to_all(x, 'seq', split_axis=0, concat_axis=0, tiled=True)]
    pallas_call x0 -> x5, Pallas kernels: none -> 131 us  [the longest x2 59.1 us: far(): pl.pallas_call(functools.partial(far_kernel, scaling, cap), grid_spec=plt...]
    all_to_all x1, blocking collectives: 11.7 us -> 121 us  [exchange(): return lax.all_to_all(x, 'seq', split_axis=0, concat_axis=0, tiled=True)]
    dynamic_update_slice x4 -> x0, local copies, waits for them, and re-layouts: 108 us -> none  [shards(): lax.scan(near_step, (zero_rows, zero_rows), (blocked(queries), blocked(gr...]
    gather x10 -> x2, local copies, waits for them, and re-layouts: 33.8 us -> 1.17 us  [task_stat(): x.reshape(heads, cubes, cube_len).transpose(1, 0, 2)]
    reduce_scatter x0 -> x1, waiting for transfers between devices: none -> 22.2 us  [shards(): lax.psum_scatter(jnp.concatenate([coarse_k, coarse_v], axis=0), 'seq', sc...]
    reshape x9 -> x5, local copies, waits for them, and re-layouts: 17.6 us -> 1.15 us  [the longest x4 1.06 us: task_stat(): x.reshape(heads, cubes, cube_len).transpose(1, 0, 2)]
  transfers between devices with their start and end apart: 5 -> 6, of which waited for: 2 -> 3; matrix products, arithmetic and copies ran while one was open for 40% -> 5% of each run, Pallas kernels for 0% -> 22%
where the time goes in v1:
time: 556 us; the launch traced here: 554 us
  blocking collectives  240 us (43%)
  Pallas kernels  131 us (24%)
  waiting for transfers between devices  100 us (18%)
  starting transfers between devices  24.8 us (4%)
  local copies, waits for them, and re-layouts  24.7 us (4%)
  other arithmetic  19.4 us (3%)
  between operations  14.3 us (3%)
    all_to_all x1, blocking collectives, exchange(): return lax.all_to_all(x, 'seq', split_axis=0, concat_axis=0, tiled=True)  121 us
    all_gather x1, blocking collectives, shards(): lax.all_gather(jnp.concatenate([pooled(keys), pooled(values)], axis=0), '...  119 us
    all_to_all x5, waiting for transfers between devices, exchange(): return lax.all_to_all(x, 'seq', split_axis=0, concat_axis=0, tiled=True)  77.9 us
    pallas_call x2, Pallas kernels, far(): pl.pallas_call(functools.partial(far_kernel, scaling, cap), grid_spec=plt...  59.1 us
    pallas_call x1, Pallas kernels, near(): pl.pallas_call(functools.partial(near_kernel, scaling, min(256, rows)), g...  40.6 us
    all_to_all x5, starting transfers between devices, exchange(): return lax.all_to_all(x, 'seq', split_axis=0, concat_axis=0, tiled=True)  24.8 us
    reduce_scatter x1, waiting for transfers between devices, shards(): lax.psum_scatter(jnp.concatenate([coarse_k, coarse_v], axis=0), 'seq', sc...  22.2 us
    pallas_call x1, Pallas kernels, pack(): pl.pallas_call(functools.partial(pack_kernel, splits), grid_spec=pltpu.Pr...  19.5 us
  transfers between devices with their start and end apart: 6, of which 3 were waited for; matrix products, arithmetic and copies ran while one was open for 5% of the time, Pallas kernels for 22%

profile of v1, /device:TPU:0, one launch (start us, length us, event | category | flops | bytes accessed | tf_op | source)
XLA Modules:
  0.0 554.4 jit_solution(4034274403955416045)
XLA Ops:
  9.5 6.3 %all-to-all-start = ((s32[4,1,8]{2,1,0:T(1,128)}), s32[4,1,8]{2,1,0:T(1,128)S(1)}, u32[]{:S(2)}, u32[]{:S(2)}) async-start(s32[4,1,8]{2,1,0:T(1,128)} %bitcast.14), calls=%async_computation | async-start | bytes 4096 | tf_op jit(solution)/shard_map/all_to_all | solution.py:230
  16.0 0.9 reshape.166
  16.9 6.1 %fusion = (f32[10,1024]{1,0:T(8,128)S(1)}, f32[10,1024]{1,0:T(8,128)S(1)}) fusion(bf16[1024,10,128]{2,0,1:T(8,128)(2,1)} %param.13, bf16[1024,10,128]{2,0,1:T(8,128)(2,1)} %param.12, bf16[1024,10,128]{2,0,1:T(8,128)(2,1)} %param.14), kind=kLoop, calls=%fused_computation.4 | loop fusion | flops 9154560 | bytes 7946240 | tf_op jit(solution)/shard_map/the,the->ht/dot_general | solution.py:262
  25.2 5.1 all-to-all-start.2
  30.3 5.8 %copy.41.do_ref = bf16[1024,10,128]{2,1,0:T(8,128)(2,1)} copy(bf16[1024,10,128]{2,0,1:T(8,128)(2,1)} %param.12) | data formatting | bytes 5242880 | tf_op args[3]
  36.2 1.9 copy.40.q_ref
  38.1 19.5 %shard_map.129 = (bf16[32,2,5,64,128]{4,3,2,1,0:T(8,128)(2,1)}, bf16[32,2,5,64,128]{4,3,2,1,0:T(8,128)(2,1)}) custom-call(s32[32]{0:T(128)S(1)} %get-tuple-element.58.task_ref, bf16[1024,10,128]{2,1,0:T(8,128)(2,1)S(1)} %copy.40.q_ref, bf16[1024,10,128]{2,1,0:T(8,128)(2,1)} %copy.41.do_ref), custom_call_target="tpu_custom_call" | custom-call | tf_op jit(solution)/shard_map/pallas_call | solution.py:50
  57.6 121.2 %all_to_all.31 = bf16[4,8,2,5,64,128]{5,4,3,2,1,0:T(8,128)(2,1)} all-to-all(bf16[4,8,2,5,64,128]{5,4,3,2,1,0:T(8,128)(2,1)} %bitcast.82), channel_id=1, replica_groups=mesh['groups'=2,'seq'=4,'head'=2,'pair'=2] {'seq'}, dimensions={0} | all-to-all | bytes 10485760 | tf_op jit(solution)/shard_map/all_to_all | solution.py:230
  178.8 5.2 all-to-all-start.1
  184.2 2.8 convert_reduce_fusion.1
  187.0 0.9 convert_reduce_fusion
  188.1 118.9 %all_gather.3 = bf16[20,64,128]{2,1,0:T(8,128)(2,1)S(1)} all-gather(bf16[20,16,128]{2,1,0:T(8,128)(2,1)S(1)} %pad_maximum_fusion.3), channel_id=1, replica_groups=mesh['groups'=2,'seq'=4,'head'=2,'pair'=2] {'seq'}, dimensions={1}, use_global_device_ids=true | all-gather | bytes 409600 | tf_op jit(solution)/shard_map/all_gather | solution.py:278
  307.1 40.6 %shard_map.128 = (f32[10,1024,128]{2,1,0:T(8,128)}, f32[10,1024,128]{2,1,0:T(8,128)}, f32[10,1024,128]{2,1,0:T(8,128)}, f32[10,64,128]{2,1,0:T(8,128)S(1)}, f32[10,64,128]{2,1,0:T(8,128)S(1)}) custom-call(bf16[10,1024,128]{2,1,0:T(8,128)(2,1)S(1)} %bitcast.74, bf16[10,1024,128]{2,1,0:T(8,128)(2,1)} %bitcast.79, bf16[10,1024,128]{2,1,0:T(8,128)(2,1)} %bitcast.83, ...), custom_call_target="tpu_custom_call" | custom-call | flops 28521267200 | bytes 26214400 | tf_op jit(solution)/shard_map/pallas_call | solution.py:96
  347.7 0.9 pad_maximum_fusion
  349.9 22.2 %reduce-scatter.2.cloned.1.call-done = f32[20,16,128]{2,1,0:T(8,128)} async-done(((f32[20,64,128]{2,1,0:T(8,128)}), f32[20,16,128]{2,1,0:T(8,128)}) %reduce-scatter.2.cloned.1.call-update) | async-done | bytes 163856 | tf_op jit(solution)/shard_map/reduce_scatter | solution.py:286
  372.1 1.6 slice_bitcast_fusion
  373.7 29.6 %shard_map.131 = (bf16[32,5,64,128]{3,2,1,0:T(8,128)(2,1)S(1)}, bf16[5,1024,128]{2,1,0:T(8,128)(2,1)S(1)}, bf16[5,1024,128]{2,1,0:T(8,128)(2,1)S(1)}) custom-call(s32[32]{0:T(128)S(1)} %reshape.163.asked_ref, bf16[32,2,5,64,128]{4,3,2,1,0:T(8,128)(2,1)} %bitcast.81, f32[10,32,128]{2,1,0:T(8,128)S(1)} %bitcast.77, bf16[10,1024,128]{2,1,0:T(8,128)(2,1)} %bitcast.84, ...), custom_call_target="tpu_custom_call" | custom-call | flops 8388608000 | bytes 19660800 | tf_op jit(solution)/shard_map/pallas_call | solution.py:161
  403.3 1.5 copy-done.1
  404.8 1.1 copy-done.3
  405.8 1.1 copy-done.5
  406.9 3.7 all-to-all-start.5
  410.6 29.5 %shard_map.130 = (bf16[32,5,64,128]{3,2,1,0:T(8,128)(2,1)S(1)}, bf16[5,1024,128]{2,1,0:T(8,128)(2,1)S(1)}, bf16[5,1024,128]{2,1,0:T(8,128)(2,1)S(1)}) custom-call(s32[32]{0:T(128)S(1)} %reshape.163.asked_ref, bf16[32,2,5,64,128]{4,3,2,1,0:T(8,128)(2,1)} %bitcast.16.got_ref, f32[10,32,128]{2,1,0:T(8,128)S(1)} %bitcast.78, bf16[10,1024,128]{2,1,0:T(8,128)(2,1)} %bitcast.85, ...), custom_call_target="tpu_custom_call" | custom-call | flops 8388608000 | bytes 19660800 | tf_op jit(solution)/shard_map/pallas_call | solution.py:161
  440.1 1.5 copy-done.2
  441.6 1.1 copy-done.6
  442.7 1.1 copy-done.8
  443.8 24.2 %all-to-all-done.5 = bf16[4,8,5,64,128]{4,3,2,1,0:T(8,128)(2,1)S(1)} async-done(((bf16[4,8,5,64,128]{4,3,2,1,0:T(8,128)(2,1)}), bf16[4,8,5,64,128]{4,3,2,1,0:T(8,128)(2,1)S(1)}, u32[]{:S(2)}, u32[]{:S(2)}) %all-to-all-start.5) | async-done | bytes 2621472 | tf_op jit(solution)/shard_map/all_to_all | solution.py:230
  468.0 4.6 all-to-all-start.3
  472.6 3.6 maximum_bitcast_fusion
  476.1 1.7 maximum_bitcast_fusion.1
  477.9 53.7 %all-to-all-done.3 = bf16[4,8,5,64,128]{4,3,2,1,0:T(8,128)(2,1)} async-done(((bf16[4,8,5,64,128]{4,3,2,1,0:T(8,128)(2,1)}), bf16[4,8,5,64,128]{4,3,2,1,0:T(8,128)(2,1)}, u32[]{:S(2)}, u32[]{:S(2)}) %all-to-all-start.3) | async-done | bytes 2621472 | tf_op jit(solution)/shard_map/all_to_all | solution.py:230
  531.5 11.7 %shard_map.132 = bf16[1024,10,128]{2,1,0:T(8,128)(2,1)} custom-call(s32[16]{0:T(128)S(1)} %multiply_add_fusion.slot_ref, f32[10,1024,128]{2,1,0:T(8,128)} %get-tuple-element.18.nq_ref, bf16[32,5,64,128]{3,2,1,0:T(8,128)(2,1)} %bitcast.26.refs_0_, bf16[32,5,64,128]{3,2,1,0:T(8,128)(2,1)S(1)} %bitcast.73), custom_call_target="tpu_custom_call" | custom-call | tf_op jit(solution)/shard_map/pallas_call | solution.py:216
  543.2 4.4 copy.47
  (54 shorter events, 6.4 us)
Async XLA Ops:
  9.5 15.7 %all-to-all-start = ((s32[4,1,8]{2,1,0:T(1,128)}), s32[4,1,8]{2,1,0:T(1,128)S(1)}, u32[]{:S(2)}, u32[]{:S(2)}) async-start(s32[4,1,8]{2,1,0:T(1,128)} %bitcast.14), calls=%async_computation | async-start | bytes 4096 | tf_op jit(solution)/shard_map/all_to_all | solution.py:230
  25.2 32.3 %all-to-all-start.2 = ((f32[4,8,10,128]{3,1,2,0:T(8,128)}), f32[4,8,10,128]{3,1,2,0:T(8,128)S(1)}, u32[]{:S(2)}, u32[]{:S(2)}) async-start(f32[4,8,10,128]{3,1,2,0:T(8,128)} %pad_maximum_fusion.2), calls=%async_computation.2 | async-start | bytes 327680 | tf_op jit(solution)/shard_map/all_to_all | solution.py:230
  30.3 5.8 %copy-start = (bf16[1024,10,128]{2,0,1:T(8,128)(2,1)S(1)}, bf16[1024,10,128]{2,0,1:T(8,128)(2,1)}, u32[]{:S(2)}) copy-start(bf16[1024,10,128]{2,0,1:T(8,128)(2,1)} %param.9) | copy-start | bytes 7864324
  178.8 5.2 copy-start.10
  178.8 5.3 copy-start.11
  178.8 228.1 %all-to-all-start.1 = ((bf16[4,8,2,5,64,128]{5,4,3,2,1,0:T(8,128)(2,1)}), bf16[4,8,2,5,64,128]{5,4,3,2,1,0:T(8,128)(2,1)}, u32[]{:S(2)}, u32[]{:S(2)}) async-start(bf16[4,8,2,5,64,128]{5,4,3,2,1,0:T(8,128)(2,1)} %bitcast.80), calls=%async_computation.1 | async-start | bytes 10485760 | tf_op jit(solution)/shard_map/all_to_all | solution.py:230
  184.0 188.1 %reduce-scatter.2.cloned.1.call-start = ((), (), s32[]{:S(2)}) async-start(), calls=%async_computation.7 | async-start | bytes 819200 | tf_op jit(solution)/shard_map/reduce_scatter | solution.py:286
  184.1 2.9 copy-start.9
  403.3 1.5 copy-start.1
  404.8 1.1 copy-start.3
  405.8 1.1 copy-start.5
  406.9 61.1 %all-to-all-start.5 = ((bf16[4,8,5,64,128]{4,3,2,1,0:T(8,128)(2,1)}), bf16[4,8,5,64,128]{4,3,2,1,0:T(8,128)(2,1)S(1)}, u32[]{:S(2)}, u32[]{:S(2)}) async-start(bf16[4,8,5,64,128]{4,3,2,1,0:T(8,128)(2,1)} %bitcast.75), calls=%async_computation.6 | async-start | bytes 5242880 | tf_op jit(solution)/shard_map/all_to_all | solution.py:230
  440.1 1.5 copy-start.2
  441.6 1.1 copy-start.6
  442.7 1.1 copy-start.8
  468.0 63.5 %all-to-all-start.3 = ((bf16[4,8,5,64,128]{4,3,2,1,0:T(8,128)(2,1)}), bf16[4,8,5,64,128]{4,3,2,1,0:T(8,128)(2,1)}, u32[]{:S(2)}, u32[]{:S(2)}) async-start(bf16[4,8,5,64,128]{4,3,2,1,0:T(8,128)(2,1)} %bitcast.76), calls=%async_computation.4 | async-start | bytes 5242880 | tf_op jit(solution)/shard_map/all_to_all | solution.py:230
  472.5 3.6 copy-start.4
  472.6 3.6 copy-start.7
Sparse Core Ops, SparseCore 0:
  348.7 23.3 reduce-scatter.1

commit v2 on v1

v2 whole, which is shorter than its diff:
```python
import functools

import jax
import jax.numpy as jnp
from jax import lax
from jax.experimental import pallas as pl
from jax.experimental.pallas import tpu as pltpu
from jax.sharding import PartitionSpec as P

F32 = jnp.float32
BF16 = jnp.bfloat16
VMEM_BYTES = 48 * 1024 * 1024
OFF_LSE = 1e30


def dot_nt(a, b):
    return lax.dot_general(a, b, (((1,), (1,)), ((), ())), preferred_element_type=F32)


def dot_nn(a, b):
    return lax.dot_general(a, b, (((1,), (0,)), ((), ())), preferred_element_type=F32)


def dot_tn(a, b):
    return lax.dot_general(a, b, (((0,), (0,)), ((), ())), preferred_element_type=F32)


def block_rule(q, do, lse, delta, k, v, scaling):
    probs = jnp.exp(dot_nt(k, q) * scaling - lse)
    dscores = (probs * (dot_nt(v, do) - delta)).astype(BF16)
    return probs.astype(BF16), dscores


def params(**more):
    return pltpu.CompilerParams(vmem_limit_bytes=VMEM_BYTES, **more)


def pack_kernel(splits, task_ref, q_ref, do_ref, *outs):
    for part, ref in ((0, q_ref), (1, do_ref)):
        flipped = jnp.swapaxes(ref[...].astype(F32), 0, 1).astype(BF16)
        for (low, high), out in zip(splits, outs):
            out[0, part] = flipped[low:high]


def pack(queries, grad_out, task_of_slot, cube_len, far_count, splits):
    _, heads, width = queries.shape
    slots = task_of_slot.shape[0]
    source = pl.BlockSpec((cube_len, heads, width), lambda s, t: (t[s] // far_count, 0, 0))
    sizes = [(2, high - low, cube_len, width) for low, high in splits]
    return pl.pallas_call(
        functools.partial(pack_kernel, splits),
        grid_spec=pltpu.PrefetchScalarGridSpec(
            num_scalar_prefetch=1,
            grid=(slots,),
            in_specs=[source, source],
            out_specs=[pl.BlockSpec((1,) + size, lambda s, t: (s, 0, 0, 0, 0)) for size in sizes],
        ),
        out_shape=[jax.ShapeDtypeStruct((slots,) + size, BF16) for size in sizes],
        compiler_params=params(),
    )(task_of_slot, queries, grad_out)


def near_kernel(
    scaling, chunk, q_ref, do_ref, k_ref, v_ref, pk_ref, pv_ref, stat_ref,
    dq_ref, dk_ref, dv_ref, ck_ref, cv_ref,
):
    rows = q_ref.shape[1]
    k, v, pk, pv = k_ref[0], v_ref[0], pk_ref[0], pv_ref[0]
    for start in range(0, rows, chunk):
        at = slice(start, start + chunk)
        q, do = q_ref[0, at, :], do_ref[0, at, :]
        fine = block_rule(q, do, stat_ref[0, 0:1, at], stat_ref[0, 1:2, at], k, v, scaling)
        coarse = block_rule(q, do, stat_ref[0, 2:3, at], stat_ref[0, 3:4, at], pk, pv, scaling)
        dq_ref[0, at, :] = scaling * (dot_tn(fine[1], k) + dot_tn(coarse[1], pk))
        for (probs, dscores), key_out, value_out in (
            (fine, dk_ref, dv_ref),
            (coarse, ck_ref, cv_ref),
        ):
            grad_k = scaling * dot_nn(dscores, q)
            grad_v = dot_nn(probs, do)
            if start == 0:
                key_out[0] = grad_k
                value_out[0] = grad_v
            else:
                key_out[0] += grad_k
                value_out[0] += grad_v


def near(q, do, k, v, pooled_k, pooled_v, stats, scaling):
    heads, rows, width = q.shape
    pooled = pooled_k.shape[1]
    token = pl.BlockSpec((1, rows, width), lambda h: (h, 0, 0))
    cube = pl.BlockSpec((1, pooled, width), lambda h: (h, 0, 0))
    token_out = jax.ShapeDtypeStruct((heads, rows, width), F32)
    cube_out = jax.ShapeDtypeStruct((heads, pooled, width), F32)
    return pl.pallas_call(
        functools.partial(near_kernel, scaling, min(256, rows)),
        grid=(heads,),
        in_specs=[token] * 4 + [cube] * 2 + [pl.BlockSpec((1, 4, rows), lambda h: (h, 0, 0))],
        out_specs=[token] * 3 + [cube] * 2,
        out_shape=[token_out] * 3 + [cube_out] * 2,
        compiler_params=params(),
        cost_estimate=pl.CostEstimate(
            flops=20 * heads * rows * (rows + pooled) * width,
            bytes_accessed=heads * rows * width * 20,
            transcendentals=heads * rows * (rows + pooled),
        ),
    )(q, do, k, v, pooled_k, pooled_v, stats)


def far_kernel(scaling, cap, steps, asked_ref, *refs):
    gots = refs[:steps]
    stat_ref, k_ref, v_ref, nk_ref, nv_ref, ok_ref, ov_ref = refs[steps : steps + 7]
    dqs = refs[steps + 7 : 2 * steps + 7]
    gk_ref, gv_ref, acc_k, acc_v = refs[2 * steps + 7 :]
    cubes, width = ok_ref.shape[1:]
    cube_len = k_ref.shape[1] // cubes
    for cube in range(cubes):
        at = slice(cube * cube_len, (cube + 1) * cube_len)
        acc_k[at, :] = nk_ref[0, at, :] + ok_ref[0, cube : cube + 1, :] * (1.0 / cube_len)
        acc_v[at, :] = nv_ref[0, at, :] + ov_ref[0, cube : cube + 1, :] * (1.0 / cube_len)
    for step in range(steps):
        pending = []
        for slot in range(cap):
            index = step * cap + slot
            first = pl.multiple_of(asked_ref[index] * cube_len, cube_len)
            at = pl.ds(first, cube_len)
            k, v = k_ref[0, at, :], v_ref[0, at, :]
            q, do = gots[step][slot, 0, 0], gots[step][slot, 1, 0]
            stat = stat_ref[0, index : index + 1, :]
            probs, dscores = block_rule(
                q, do, stat[:, :cube_len], stat[:, cube_len:], k, v, scaling
            )
            dqs[step][slot, 0] = (scaling * dot_tn(dscores, k)).astype(BF16)
            task_k = (scaling * dot_nn(dscores, q)).astype(BF16)
            task_v = dot_nn(probs, do).astype(BF16)
            pending.append((at, task_k, task_v))
        for at, task_k, task_v in pending:
            acc_k[at, :] += task_k.astype(F32)
            acc_v[at, :] += task_v.astype(F32)
    gk_ref[0] = acc_k[...].astype(BF16)
    gv_ref[0] = acc_v[...].astype(BF16)


def far(asked, gots, stats, k, v, near_k, near_v, own_k, own_v, low, scaling):
    steps = len(gots)
    cap, _, heads, cube_len, width = gots[0].shape
    slots = steps * cap
    rows = k.shape[1]
    cubes = own_k.shape[1]
    token = pl.BlockSpec((1, rows, width), lambda h, a: (h + low, 0, 0))
    cube = pl.BlockSpec((1, cubes, width), lambda h, a: (h + low, 0, 0))
    out = pl.BlockSpec((1, rows, width), lambda h, a: (h, 0, 0))
    got = pl.BlockSpec((cap, 2, 1, cube_len, width), lambda h, a: (0, 0, h, 0, 0))
    dq = pl.BlockSpec((cap, 1, cube_len, width), lambda h, a: (0, h, 0, 0))
    results = pl.pallas_call(
        functools.partial(far_kernel, scaling, cap, steps),
        grid_spec=pltpu.PrefetchScalarGridSpec(
            num_scalar_prefetch=1,
            grid=(heads,),
            in_specs=[got] * steps
            + [pl.BlockSpec((1, slots, 2 * cube_len), lambda h, a: (h + low, 0, 0))]
            + [token] * 4
            + [cube] * 2,
            out_specs=[dq] * steps + [out] * 2,
            scratch_shapes=[pltpu.VMEM((rows, width), F32)] * 2,
        ),
        out_shape=[jax.ShapeDtypeStruct((cap, heads, cube_len, width), BF16)] * steps
        + [jax.ShapeDtypeStruct((heads, rows, width), BF16)] * 2,
        compiler_params=params(),
        cost_estimate=pl.CostEstimate(
            flops=100 * heads * slots * cube_len * cube_len * width,
            bytes_accessed=heads * rows * width * 30,
            transcendentals=heads * slots * cube_len * cube_len,
        ),
    )(asked, *gots, stats, k, v, near_k, near_v, own_k, own_v)
    return results[:steps], results[steps], results[steps + 1]


def join_kernel(splits, steps, cap, far_count, slot_ref, nq_ref, *refs):
    out = refs[-1]
    pieces = iter(refs[:-1])
    cube = pl.program_id(0)
    total = []
    for low, high in splits:
        piece = nq_ref[low:high]
        for step in range(steps):
            for far_at in range(far_count):
                slot = slot_ref[cube * far_count + far_at]
                here = (slot >= step * cap) & (slot < (step + 1) * cap)
                piece = piece + jnp.where(here, next(pieces)[0].astype(F32), 0.0)
        total.append(piece)
    out[...] = jnp.swapaxes(jnp.concatenate(total, axis=0), 0, 1).astype(BF16)


def join(near_q, back, slot_of_task, cube_len, far_count, splits):
    heads, rows, width = near_q.shape
    steps, cap = len(back[0]), back[0][0].shape[0]
    specs, operands = [], []
    for (low, high), arrays in zip(splits, back):
        for step in range(steps):
            for far_at in range(far_count):

                def place(c, s, step=step, far_at=far_at):
                    slot = s[c * far_count + far_at] - step * cap
                    return (jnp.clip(slot, 0, cap - 1), 0, 0, 0)

                specs.append(pl.BlockSpec((1, high - low, cube_len, width), place))
                operands.append(arrays[step])
    return pl.pallas_call(
        functools.partial(join_kernel, splits, steps, cap, far_count),
        grid_spec=pltpu.PrefetchScalarGridSpec(
            num_scalar_prefetch=1,
            grid=(rows // cube_len,),
            in_specs=[pl.BlockSpec((heads, cube_len, width), lambda c, s: (0, c, 0))] + specs,
            out_specs=pl.BlockSpec((cube_len, heads, width), lambda c, s: (c, 0, 0)),
        ),
        out_shape=jax.ShapeDtypeStruct((rows, heads, width), BF16),
        compiler_params=params(),
    )(slot_of_task, near_q, *operands)


def shift(x, step):
    size = lax.axis_size("seq")
    return lax.ppermute(x, "seq", [(i, (i + step) % size) for i in range(size)])


def shards(queries, keys, values, grad_out, fine_out, coarse_out, fine_lse, coarse_lse, select):
    rows, heads, width = queries.shape
    cubes, far_count = select.shape
    cube_len = rows // cubes
    scaling = width ** (-0.5)
    seq_size = lax.axis_size("seq")
    cap = max(2, min(cubes * far_count // 2, 3 * cubes * far_count // seq_size))
    steps = seq_size - 1
    slots = steps * cap
    tasks = cubes * far_count
    half = heads // 2
    splits = ((0, half), (half, heads))
    me = lax.axis_index("seq")

    targets = select.reshape(-1)
    away = (targets // cubes - me + seq_size) % seq_size
    local_cube = targets % cubes
    task_index = jnp.arange(tasks, dtype=jnp.int32)
    earlier = (away[None, :] == away[:, None]) & (task_index[None, :] < task_index[:, None])
    slot_of_task = (away - 1) * cap + jnp.sum(earlier.astype(jnp.int32), axis=1)
    matches = slot_of_task[None, :] == jnp.arange(slots, dtype=jnp.int32)[:, None]
    occupied = jnp.any(matches, axis=1)
    task_of_slot = jnp.sum(jnp.where(matches, task_index[None, :], 0), axis=1)
    cube_of_slot = jnp.sum(jnp.where(matches, local_cube[None, :], 0), axis=1)

    def of_step(x, step):
        return x[step * cap : (step + 1) * cap]

    sends = [
        pack(queries, grad_out, of_step(task_of_slot, s), cube_len, far_count, splits)
        for s in range(steps)
    ]
    first = [shift(sends[s][0], s + 1) for s in range(steps)]

    def pooled(x):
        mean = jnp.mean(x.reshape(cubes, cube_len, heads, width), axis=1, dtype=F32)
        return mean.astype(BF16).transpose(1, 0, 2)

    own_pooled = jnp.concatenate([pooled(keys), pooled(values)], axis=0)
    all_pooled = jnp.concatenate(
        [own_pooled] + [shift(own_pooled, -s) for s in range(1, seq_size)], axis=1
    )

    delta_fine = jnp.einsum("the,the->ht", grad_out, fine_out, preferred_element_type=F32)
    delta_coarse = jnp.einsum("the,the->ht", grad_out, coarse_out, preferred_element_type=F32)

    def task_stat(x):
        return x.reshape(heads, cubes, cube_len).transpose(1, 0, 2)[task_of_slot // far_count]

    slot_lse = jnp.where(occupied[:, None, None], task_stat(fine_lse), OFF_LSE)
    slot_stats = jnp.concatenate([slot_lse, task_stat(delta_fine)], axis=2)
    slot_cube = jnp.broadcast_to(
        cube_of_slot.astype(F32)[:, None, None], (slots, 1, 2 * cube_len)
    )
    slot_stats = jnp.concatenate([slot_stats, slot_cube], axis=1)
    got_stats = jnp.concatenate([shift(of_step(slot_stats, s), s + 1) for s in range(steps)], axis=0)
    asked = got_stats[:, heads, 0].astype(jnp.int32)
    got_stats = got_stats[:, :heads].transpose(1, 0, 2)

    q, do, k, v = (x.transpose(1, 0, 2) for x in (queries, grad_out, keys, values))
    stats = jnp.stack([fine_lse, delta_fine, coarse_lse, delta_coarse], axis=1)
    near_q, near_k, near_v, coarse_k, coarse_v = near(
        q, do, k, v, all_pooled[:heads], all_pooled[heads:], stats, scaling
    )

    coarse = jnp.concatenate([coarse_k, coarse_v], axis=0)
    own = coarse[:, :cubes]
    for s in range(1, seq_size):
        own = own + shift(coarse[:, s * cubes : (s + 1) * cubes], s)
    own_k, own_v = own[:heads], own[heads:]

    later = [send[1] for send in sends]
    first, later = lax.optimization_barrier((first, later))
    second = [shift(later[s], s + 1) for s in range(steps)]

    back, grads_k, grads_v = [], [], []
    for (low, high), gots in zip(splits, (first, second)):
        task_q, grad_k, grad_v = far(
            asked, gots, got_stats, k, v, near_k, near_v, own_k, own_v, low, scaling
        )
        back.append([shift(task_q[s], -(s + 1)) for s in range(steps)])
        grads_k.append(grad_k)
        grads_v.append(grad_v)
    grad_queries = join(near_q, back, slot_of_task, cube_len, far_count, splits)
    grad_keys = jnp.concatenate(grads_k, axis=0).transpose(1, 0, 2)
    grad_values = jnp.concatenate(grads_v, axis=0).transpose(1, 0, 2)
    return (
        grad_queries,
        grad_keys,
        grad_values,
        own_k.transpose(1, 0, 2),
        own_v.transpose(1, 0, 2),
    )


def solution(mesh):
    token = P(("groups", "seq"), ("head", "pair"), None)
    stat = P(("head", "pair"), ("groups", "seq"))
    return jax.shard_map(
        shards,
        mesh=mesh,
        in_specs=(token,) * 6 + (stat, stat, P(("groups", "seq"), None)),
        out_specs=(token,) * 5,
        check_vma=False,
    )
```

time: 556 us -> 423 us (0.76)
  blocking collectives: 240 us -> 0 us
  starting transfers between devices: 24.8 us -> 123 us
  waiting for transfers between devices: 100 us -> 140 us
  between operations: 14.3 us -> 0.97 us
  local copies, waits for them, and re-layouts: 24.7 us -> 17.3 us
  Pallas kernels: 131 us -> 124 us
    ppermute x0 -> x21, waiting for transfers between devices: none -> 140 us  [shift(): return lax.ppermute(x, 'seq', [(i, (i + step) % size) for i in range(size)])]
    ppermute x0 -> x21, starting transfers between devices: none -> 123 us  [shift(): return lax.ppermute(x, 'seq', [(i, (i + step) % size) for i in range(size)])]
    all_to_all x1 -> x0, blocking collectives: 121 us -> none  [exchange(): return lax.all_to_all(x, 'seq', split_axis=0, concat_axis=0, tiled=True)]
    all_gather x1 -> x0, blocking collectives: 119 us -> none  [shards(): lax.all_gather(jnp.concatenate([pooled(keys), pooled(values)], axis=0), '...]
    all_to_all x5 -> x0, waiting for transfers between devices: 77.9 us -> none  [exchange(): return lax.all_to_all(x, 'seq', split_axis=0, concat_axis=0, tiled=True)]
    all_to_all x5 -> x0, starting transfers between devices: 24.8 us -> none  [exchange(): return lax.all_to_all(x, 'seq', split_axis=0, concat_axis=0, tiled=True)]
    reduce_scatter x1 -> x0, waiting for transfers between devices: 22.2 us -> none  [shards(): lax.psum_scatter(jnp.concatenate([coarse_k, coarse_v], axis=0), 'seq', sc...]
    unnamed x27 -> x22, local copies, waits for them, and re-layouts: 19.4 us -> 13.2 us
  transfers between devices with their start and end apart: 6 -> 21, of which waited for: 3 -> 4; matrix products, arithmetic and copies ran while one was open for 5% -> 5% of each run, Pallas kernels for 22% -> 27%
where the time goes in v2:
time: 423 us; the launch traced here: 421 us
  waiting for transfers between devices  140 us (33%)
  Pallas kernels  124 us (29%)
  starting transfers between devices  123 us (29%)
  local copies, waits for them, and re-layouts  17.3 us (4%)
  other arithmetic  15.1 us (4%)
    ppermute x21, waiting for transfers between devices, shift(): return lax.ppermute(x, 'seq', [(i, (i + step) % size) for i in range(size)])  140 us
    ppermute x21, starting transfers between devices, shift(): return lax.ppermute(x, 'seq', [(i, (i + step) % size) for i in range(size)])  123 us
    pallas_call x2, Pallas kernels, far(): pl.pallas_call(functools.partial(far_kernel, scaling, cap, steps), grid_s...  55.8 us
    pallas_call x1, Pallas kernels, near(): pl.pallas_call(functools.partial(near_kernel, scaling, min(256, rows)), g...  40.7 us
    pallas_call x3, Pallas kernels, pack(): pl.pallas_call(functools.partial(pack_kernel, splits), grid_spec=pltpu.Pr...  15.8 us
    unnamed x22, local copies, waits for them, and re-layouts  13.2 us
    pallas_call x1, Pallas kernels, join(): pl.pallas_call(functools.partial(join_kernel, splits, steps, cap, far_cou...  12.1 us
  transfers between devices with their start and end apart: 21, of which 4 were waited for; matrix products, arithmetic and copies ran while one was open for 5% of the time, Pallas kernels for 27%

profile of v2, /device:TPU:0, one launch (start us, length us, event | category | flops | bytes accessed | tf_op | source)
XLA Modules:
  0.0 421.2 jit_solution(12844699537777726694)
XLA Ops:
  0.7 2.8 convert_reduce_fusion.1
  3.5 0.9 convert_reduce_fusion
  5.1 3.0 collective-permute-start.2
  8.1 2.6 collective-permute-start.1
  10.7 1.3 collective-permute-start
  12.6 5.4 %fusion = (f32[10,1024]{1,0:T(8,128)S(1)}, f32[10,1024]{1,0:T(8,128)S(1)}) fusion(bf16[1024,10,128]{2,0,1:T(8,128)(2,1)} %param.13, bf16[1024,10,128]{2,0,1:T(8,128)(2,1)S(1)} %copy-done.1, bf16[1024,10,128]{2,0,1:T(8,128)(2,1)} %param.14), kind=kLoop, calls=%fused_computation.4 | loop fusion | flops 9154560 | bytes 7946240 | tf_op jit(solution)/shard_map/the,the->ht/dot_general | solution.py:271
  20.1 1.6 collective-permute-start.3
  23.7 3.9 copy.47.do_ref
  27.6 3.8 copy.46.q_ref
  31.5 6.8 %shard_map.131 = (bf16[8,2,5,64,128]{4,3,2,1,0:T(8,128)(2,1)}, bf16[8,2,5,64,128]{4,3,2,1,0:T(8,128)(2,1)S(1)}) custom-call(s32[8]{0:T(128)S(1)} %get-tuple-element.95.task_ref, bf16[1024,10,128]{2,1,0:T(8,128)(2,1)} %copy.46.q_ref, bf16[1024,10,128]{2,1,0:T(8,128)(2,1)} %copy.47.do_ref), custom_call_target="tpu_custom_call" | custom-call | tf_op jit(solution)/shard_map/pallas_call | solution.py:50
  38.2 4.1 shard_map.130
  42.3 4.9 %shard_map.129 = (bf16[8,2,5,64,128]{4,3,2,1,0:T(8,128)(2,1)S(1)}, bf16[8,2,5,64,128]{4,3,2,1,0:T(8,128)(2,1)S(1)}) custom-call(s32[8]{0:T(128)S(1)} %get-tuple-element.97.task_ref, bf16[1024,10,128]{2,1,0:T(8,128)(2,1)} %copy.46.q_ref, bf16[1024,10,128]{2,1,0:T(8,128)(2,1)} %copy.47.do_ref), custom_call_target="tpu_custom_call" | custom-call | tf_op jit(solution)/shard_map/pallas_call | solution.py:50
  47.9 3.2 collective-permute-start.8
  52.4 1.0 pad_maximum_fusion
  53.4 40.7 %shard_map.128 = (f32[10,1024,128]{2,1,0:T(8,128)}, f32[10,1024,128]{2,1,0:T(8,128)}, f32[10,1024,128]{2,1,0:T(8,128)}, f32[10,64,128]{2,1,0:T(8,128)S(1)}, f32[10,64,128]{2,1,0:T(8,128)S(1)}) custom-call(bf16[10,1024,128]{2,1,0:T(8,128)(2,1)S(1)} %bitcast.61, bf16[10,1024,128]{2,1,0:T(8,128)(2,1)} %bitcast.62, bf16[10,1024,128]{2,1,0:T(8,128)(2,1)} %bitcast.63, ...), custom_call_target="tpu_custom_call" | custom-call | flops 28521267200 | bytes 26214400 | tf_op jit(solution)/shard_map/pallas_call | solution.py:96
  94.2 11.7 %collective-permute-start.9 = (f32[20,16,128]{2,1,0:T(8,128)S(1)}, f32[20,16,128]{2,1,0:T(8,128)S(1)}, u32[]{:S(2)}, u32[]{:S(2)}) collective-permute-start(f32[20,16,128]{2,1,0:T(8,128)S(1)} %get-tuple-element.83), channel_id=1, source_target_pairs={{0,4},{4,8},{8,12},{12,0},{1,5},{5,9},{9,13},{13,1},{2,6},{6,10},{... | collective-permute-start | bytes 491528 | tf_op jit(solution)/shard_map/ppermute | solution.py:225
  105.9 3.4 collective-permute-start.11
  109.3 33.0 %collective-permute-start.10 = (f32[20,16,128]{2,1,0:T(8,128)S(1)}, f32[20,16,128]{2,1,0:T(8,128)S(1)}, u32[]{:S(2)}, u32[]{:S(2)}) collective-permute-start(f32[20,16,128]{2,1,0:T(8,128)S(1)} %get-tuple-element.85), channel_id=1, source_target_pairs={{0,8},{4,12},{8,0},{12,4},{1,9},{5,13},{9,1},{13,5},{2,10},{6,14},... | collective-permute-start | bytes 491528 | tf_op jit(solution)/shard_map/ppermute | solution.py:225
  142.3 30.9 %collective-permute-done.7.refs_1_ = bf16[8,2,5,64,128]{4,3,2,1,0:T(8,128)(2,1)S(1)} collective-permute-done((bf16[8,2,5,64,128]{4,3,2,1,0:T(8,128)(2,1)S(1)}, bf16[8,2,5,64,128]{4,3,2,1,0:T(8,128)(2,1)S(1)}, u32[]{:S(2)}, u32[]{:S(2)}) %collective-permute-start.7) | collective-permute-done | bytes 1310752 | tf_op jit(solution)/shard_map/ppermute | solution.py:225
  173.5 3.7 collective-permute-start.17
  177.2 59.3 %collective-permute-done.10 = f32[20,16,128]{2,1,0:T(8,128)S(1)} collective-permute-done((f32[20,16,128]{2,1,0:T(8,128)S(1)}, f32[20,16,128]{2,1,0:T(8,128)S(1)}, u32[]{:S(2)}, u32[]{:S(2)}) %collective-permute-start.10) | collective-permute-done | bytes 163872 | tf_op jit(solution)/shard_map/ppermute | solution.py:225
  237.3 28.2 %shard_map.132 = (bf16[8,5,64,128]{3,2,1,0:T(8,128)(2,1)}, bf16[8,5,64,128]{3,2,1,0:T(8,128)(2,1)S(1)}, bf16[8,5,64,128]{3,2,1,0:T(8,128)(2,1)S(1)}, bf16[5,1024...) custom-call(s32[24]{0:T(128)S(1)} %fusion.6.asked_ref, bf16[8,2,5,64,128]{4,3,2,1,0:T(8,128)(2,1)S(1)} %collective-permute-done.6.refs_0_, ...), custom_call_target="tpu_custom_call" | custom-call | flops 6291456000 | bytes 19660800 | tf_op jit(solution)/shard_map/pallas_call | solution.py:156
  265.5 19.6 %collective-permute-start.14 = (bf16[8,5,64,128]{3,2,1,0:T(8,128)(2,1)S(1)}, bf16[8,5,64,128]{3,2,1,0:T(8,128)(2,1)S(1)}, u32[]{:S(2)}, u32[]{:S(2)}) collective-permute-start(bf16[8,5,64,128]{3,2,1,0:T(8,128)(2,1)S(1)} %get-tuple-element.48), channel_id=1, source_target_pairs={{0,4},{4,8},{8,12},{12,0},{1,5},{5,9},{9,13},{13,1},{2,6},{6,10},{... | collective-permute-start | bytes 1966088 | tf_op jit(solution)/shard_map/ppermute | solution.py:225
  285.1 1.1 copy-done.7
  286.2 27.6 %shard_map.133 = (bf16[8,5,64,128]{3,2,1,0:T(8,128)(2,1)S(1)}, bf16[8,5,64,128]{3,2,1,0:T(8,128)(2,1)S(1)}, bf16[8,5,64,128]{3,2,1,0:T(8,128)(2,1)S(1)}, bf16[5,...) custom-call(s32[24]{0:T(128)S(1)} %fusion.6.asked_ref, ...), custom_call_target="tpu_custom_call" | custom-call | flops 6291456000 | bytes 19660800 | tf_op jit(solution)/shard_map/pallas_call | solution.py:156
  313.8 36.9 %collective-permute-start.18 = (bf16[8,5,64,128]{3,2,1,0:T(8,128)(2,1)S(1)}, bf16[8,5,64,128]{3,2,1,0:T(8,128)(2,1)S(1)}, u32[]{:S(2)}, u32[]{:S(2)}) collective-permute-start(bf16[8,5,64,128]{3,2,1,0:T(8,128)(2,1)S(1)} %get-tuple-element.52), channel_id=1, source_target_pairs={{0,12},{4,0},{8,4},{12,8},{1,13},{5,1},{9,5},{13,9},{2,14},{6,2},{... | collective-permute-start | bytes 1966088 | tf_op jit(solution)/shard_map/ppermute | solution.py:225
  351.3 1.7 maximum_bitcast_fusion
  353.0 1.7 maximum_bitcast_fusion.1
  354.8 11.1 %collective-permute-done.18.refs_3_ = bf16[8,5,64,128]{3,2,1,0:T(8,128)(2,1)S(1)} collective-permute-done((bf16[8,5,64,128]{3,2,1,0:T(8,128)(2,1)S(1)}, bf16[8,5,64,128]{3,2,1,0:T(8,128)(2,1)S(1)}, u32[]{:S(2)}, u32[]{:S(2)}) %collective-permute-start.18) | collective-permute-done | bytes 655392 | tf_op jit(solution)/shard_map/ppermute | solution.py:225
  365.9 38.7 %collective-permute-done.19.refs_4_ = bf16[8,5,64,128]{3,2,1,0:T(8,128)(2,1)S(1)} collective-permute-done((bf16[8,5,64,128]{3,2,1,0:T(8,128)(2,1)S(1)}, bf16[8,5,64,128]{3,2,1,0:T(8,128)(2,1)S(1)}, u32[]{:S(2)}, u32[]{:S(2)}) %collective-permute-start.19) | collective-permute-done | bytes 655392 | tf_op jit(solution)/shard_map/ppermute | solution.py:225
  404.7 12.1 %shard_map.134 = bf16[1024,10,128]{2,1,0:T(8,128)(2,1)} custom-call(s32[16]{0:T(128)S(1)} %multiply_add_fusion.slot_ref, f32[10,1024,128]{2,1,0:T(8,128)} %get-tuple-element.32.nq_ref, bf16[8,5,64,128]{3,2,1,0:T(8,128)(2,1)S(1)} %collective-permute-done.12.refs_0_, bf16[8,5,64,128]{3,2,1,0:T(8,128)(2,1)S(1)} %collective-permute-done.13.refs_1_, ...), custom_call_target="tpu_custom_call" | custom-call | tf_op jit(solution)/shard_map/pallas_call | solution.py:210
  416.8 4.4 %copy.52 = bf16[1024,10,128]{2,0,1:T(8,128)(2,1)} copy(bf16[1024,10,128]{2,1,0:T(8,128)(2,1)} %shard_map.134) | data formatting | bytes 5242880
  (81 shorter events, 9.1 us)
Async XLA Ops:
  0.6 2.8 copy-start.2
  0.6 11.4 %copy-start.4 = (s32[16,1]{0,1:T(1,128)S(1)}, s32[16,1]{0,1:T(1,128)}, u32[]{:S(2)}) copy-start(s32[16,1]{0,1:T(1,128)} %param.17) | copy-start | bytes 196
  0.7 11.8 %copy-start.3 = (f32[10,1024]{1,0:T(8,128)S(1)}, f32[10,1024]{1,0:T(8,128)}, u32[]{:S(2)}) copy-start(f32[10,1024]{1,0:T(8,128)} %param.15) | copy-start | bytes 122884
  0.7 11.9 %copy-start.1 = (bf16[1024,10,128]{2,0,1:T(8,128)(2,1)S(1)}, bf16[1024,10,128]{2,0,1:T(8,128)(2,1)}, u32[]{:S(2)}) copy-start(bf16[1024,10,128]{2,0,1:T(8,128)(2,1)} %param.12) | copy-start | bytes 7864324
  5.1 42.8 %collective-permute-start.2 = (bf16[20,16,128]{2,1,0:T(8,128)(2,1)}, bf16[20,16,128]{2,1,0:T(8,128)(2,1)}, u32[]{:S(2)}, u32[]{:S(2)}) collective-permute-start(bf16[20,16,128]{2,1,0:T(8,128)(2,1)} %pad_maximum_fusion.3), channel_id=1, source_target_pairs={{0,4},{4,8},{8,12},{12,0},{1,5},{5,9},{9,13},{13,1},{2,6},{6,10},{... | collective-permute-start | bytes 245768 | tf_op jit(solution)/shard_map/ppermute | solution.py:225
  8.1 43.1 %collective-permute-start.1 = (bf16[20,16,128]{2,1,0:T(8,128)(2,1)}, bf16[20,16,128]{2,1,0:T(8,128)(2,1)}, u32[]{:S(2)}, u32[]{:S(2)}) collective-permute-start(bf16[20,16,128]{2,1,0:T(8,128)(2,1)} %pad_maximum_fusion.3), channel_id=1, source_target_pairs={{0,8},{4,12},{8,0},{12,4},{1,9},{5,13},{9,1},{13,5},{2,10},{6,14},... | collective-permute-start | bytes 245768 | tf_op jit(solution)/shard_map/ppermute | solution.py:225
  10.7 41.4 %collective-permute-start = (bf16[20,16,128]{2,1,0:T(8,128)(2,1)}, bf16[20,16,128]{2,1,0:T(8,128)(2,1)}, u32[]{:S(2)}, u32[]{:S(2)}) collective-permute-start(bf16[20,16,128]{2,1,0:T(8,128)(2,1)} %pad_maximum_fusion.3), channel_id=1, source_target_pairs={{0,12},{4,0},{8,4},{12,8},{1,13},{5,1},{9,5},{13,9},{2,14},{6,2},{... | collective-permute-start | bytes 245768 | tf_op jit(solution)/shard_map/ppermute | solution.py:225
  19.6 86.3 %collective-permute-start.5 = (f32[8,11,128]{2,0,1:T(8,128)S(1)}, f32[8,11,128]{2,0,1:T(8,128)S(1)}, u32[]{:S(2)}, u32[]{:S(2)}) collective-permute-start(f32[8,11,128]{2,0,1:T(8,128)S(1)} %get-tuple-element.92), channel_id=1, source_target_pairs={{0,12},{4,0},{8,4},{12,8},{1,13},{5,1},{9,5},{13,9},{2,14},{6,2},{... | collective-permute-start | bytes 135176 | tf_op jit(solution)/shard_map/ppermute | solution.py:225
  20.1 27.2 %collective-permute-start.3 = (f32[8,11,128]{2,0,1:T(8,128)S(1)}, f32[8,11,128]{2,0,1:T(8,128)S(1)}, u32[]{:S(2)}, u32[]{:S(2)}) collective-permute-start(f32[8,11,128]{2,0,1:T(8,128)S(1)} %get-tuple-element.94), channel_id=1, source_target_pairs={{0,4},{4,8},{8,12},{12,0},{1,5},{5,9},{9,13},{13,1},{2,6},{6,10},{... | collective-permute-start | bytes 135176 | tf_op jit(solution)/shard_map/ppermute | solution.py:225
  23.7 3.9 copy-start
  47.3 46.9 %collective-permute-start.4 = (f32[8,11,128]{2,0,1:T(8,128)S(1)}, f32[8,11,128]{2,0,1:T(8,128)S(1)}, u32[]{:S(2)}, u32[]{:S(2)}) collective-permute-start(f32[8,11,128]{2,0,1:T(8,128)S(1)} %get-tuple-element.93), channel_id=1, source_target_pairs={{0,8},{4,12},{8,0},{12,4},{1,9},{5,13},{9,1},{13,5},{2,10},{6,14},... | collective-permute-start | bytes 135176 | tf_op jit(solution)/shard_map/ppermute | solution.py:225
  47.9 61.4 %collective-permute-start.8 = (bf16[8,2,5,64,128]{4,3,2,1,0:T(8,128)(2,1)}, bf16[8,2,5,64,128]{4,3,2,1,0:T(8,128)(2,1)S(1)}, u32[]{:S(2)}, u32[]{:S(2)}) collective-permute-start(bf16[8,2,5,64,128]{4,3,2,1,0:T(8,128)(2,1)} %get-tuple-element.35), channel_id=1, source_target_pairs={{0,12},{4,0},{8,4},{12,8},{1,13},{5,1},{9,5},{13,9},{2,14},{6,2},{... | collective-permute-start | bytes 3932168 | tf_op jit(solution)/shard_map/ppermute | solution.py:225
  51.2 122.1 %collective-permute-start.7 = (bf16[8,2,5,64,128]{4,3,2,1,0:T(8,128)(2,1)S(1)}, bf16[8,2,5,64,128]{4,3,2,1,0:T(8,128)(2,1)S(1)}, u32[]{:S(2)}, u32[]{:S(2)}) collective-permute-start(bf16[8,2,5,64,128]{4,3,2,1,0:T(8,128)(2,1)S(1)} %get-tuple-element.34), channel_id=1, source_target_pairs={{0,8},{4,12},{8,0},{12,4},{1,9},{5,13},{9,1},{13,5},{2,10},{6,14},... | collective-permute-start | bytes 3932168 | tf_op jit(solution)/shard_map/ppermute | solution.py:225
  52.0 121.2 %collective-permute-start.6 = (bf16[8,2,5,64,128]{4,3,2,1,0:T(8,128)(2,1)S(1)}, bf16[8,2,5,64,128]{4,3,2,1,0:T(8,128)(2,1)S(1)}, u32[]{:S(2)}, u32[]{:S(2)}) collective-permute-start(bf16[8,2,5,64,128]{4,3,2,1,0:T(8,128)(2,1)S(1)} %get-tuple-element.33), channel_id=1, source_target_pairs={{0,4},{4,8},{8,12},{12,0},{1,5},{5,9},{9,13},{13,1},{2,6},{6,10},{... | collective-permute-start | bytes 3932168 | tf_op jit(solution)/shard_map/ppermute | solution.py:225
  94.2 79.2 %collective-permute-start.9 = (f32[20,16,128]{2,1,0:T(8,128)S(1)}, f32[20,16,128]{2,1,0:T(8,128)S(1)}, u32[]{:S(2)}, u32[]{:S(2)}) collective-permute-start(f32[20,16,128]{2,1,0:T(8,128)S(1)} %get-tuple-element.83), channel_id=1, source_target_pairs={{0,4},{4,8},{8,12},{12,0},{1,5},{5,9},{9,13},{13,1},{2,6},{6,10},{... | collective-permute-start | bytes 491528 | tf_op jit(solution)/shard_map/ppermute | solution.py:225
  105.9 71.3 %collective-permute-start.11 = (f32[20,16,128]{2,1,0:T(8,128)S(1)}, f32[20,16,128]{2,1,0:T(8,128)S(1)}, u32[]{:S(2)}, u32[]{:S(2)}) collective-permute-start(f32[20,16,128]{2,1,0:T(8,128)S(1)} %get-tuple-element.84), channel_id=1, source_target_pairs={{0,12},{4,0},{8,4},{12,8},{1,13},{5,1},{9,5},{13,9},{2,14},{6,2},{... | collective-permute-start | bytes 491528 | tf_op jit(solution)/shard_map/ppermute | solution.py:225
  109.3 127.9 %copy-start.5 = (bf16[8,2,5,64,128]{4,3,2,1,0:T(8,128)(2,1)}, bf16[8,2,5,64,128]{4,3,2,1,0:T(8,128)(2,1)S(1)}, u32[]{:S(2)}) copy-start(bf16[8,2,5,64,128]{4,3,2,1,0:T(8,128)(2,1)S(1)} %collective-permute-done.8.refs_2_) | copy-start | bytes 3932164
  109.3 127.2 %collective-permute-start.10 = (f32[20,16,128]{2,1,0:T(8,128)S(1)}, f32[20,16,128]{2,1,0:T(8,128)S(1)}, u32[]{:S(2)}, u32[]{:S(2)}) collective-permute-start(f32[20,16,128]{2,1,0:T(8,128)S(1)} %get-tuple-element.85), channel_id=1, source_target_pairs={{0,8},{4,12},{8,0},{12,4},{1,9},{5,13},{9,1},{13,5},{2,10},{6,14},... | collective-permute-start | bytes 491528 | tf_op jit(solution)/shard_map/ppermute | solution.py:225
  173.3 64.0 %copy-start.6 = (bf16[8,2,5,64,128]{4,3,2,1,0:T(8,128)(2,1)}, bf16[8,2,5,64,128]{4,3,2,1,0:T(8,128)(2,1)S(1)}, u32[]{:S(2)}) copy-start(bf16[8,2,5,64,128]{4,3,2,1,0:T(8,128)(2,1)S(1)} %collective-permute-done.7.refs_1_) | copy-start | bytes 3932164
  173.3 92.2 %collective-permute-start.15 = (bf16[8,2,5,64,128]{4,3,2,1,0:T(8,128)(2,1)S(1)}, bf16[8,2,5,64,128]{4,3,2,1,0:T(8,128)(2,1)S(1)}, u32[]{:S(2)}, u32[]{:S(2)}) collective-permute-start(bf16[8,2,5,64,128]{4,3,2,1,0:T(8,128)(2,1)S(1)} %get-tuple-element.49), channel_id=1, source_target_pairs={{0,4},{4,8},{8,12},{12,0},{1,5},{5,9},{9,13},{13,1},{2,6},{6,10},{... | collective-permute-start | bytes 3932168 | tf_op jit(solution)/shard_map/ppermute | solution.py:225
  173.3 111.9 %collective-permute-start.16 = (bf16[8,2,5,64,128]{4,3,2,1,0:T(8,128)(2,1)S(1)}, bf16[8,2,5,64,128]{4,3,2,1,0:T(8,128)(2,1)S(1)}, u32[]{:S(2)}, u32[]{:S(2)}) collective-permute-start(bf16[8,2,5,64,128]{4,3,2,1,0:T(8,128)(2,1)S(1)} %get-tuple-element.50), channel_id=1, source_target_pairs={{0,8},{4,12},{8,0},{12,4},{1,9},{5,13},{9,1},{13,5},{2,10},{6,14},... | collective-permute-start | bytes 3932168 | tf_op jit(solution)/shard_map/ppermute | solution.py:225
  173.5 112.8 %collective-permute-start.17 = (bf16[8,2,5,64,128]{4,3,2,1,0:T(8,128)(2,1)S(1)}, bf16[8,2,5,64,128]{4,3,2,1,0:T(8,128)(2,1)}, u32[]{:S(2)}, u32[]{:S(2)}) collective-permute-start(bf16[8,2,5,64,128]{4,3,2,1,0:T(8,128)(2,1)S(1)} %get-tuple-element.51), channel_id=1, source_target_pairs={{0,12},{4,0},{8,4},{12,8},{1,13},{5,1},{9,5},{13,9},{2,14},{6,2},{... | collective-permute-start | bytes 3932168 | tf_op jit(solution)/shard_map/ppermute | solution.py:225
  265.4 85.2 %collective-permute-start.12 = (bf16[8,5,64,128]{3,2,1,0:T(8,128)(2,1)}, bf16[8,5,64,128]{3,2,1,0:T(8,128)(2,1)S(1)}, u32[]{:S(2)}, u32[]{:S(2)}) collective-permute-start(bf16[8,5,64,128]{3,2,1,0:T(8,128)(2,1)} %get-tuple-element.46), channel_id=1, source_target_pairs={{0,12},{4,0},{8,4},{12,8},{1,13},{5,1},{9,5},{13,9},{2,14},{6,2},{... | collective-permute-start | bytes 1966088 | tf_op jit(solution)/shard_map/ppermute | solution.py:225
  265.4 89.3 %collective-permute-start.13 = (bf16[8,5,64,128]{3,2,1,0:T(8,128)(2,1)S(1)}, bf16[8,5,64,128]{3,2,1,0:T(8,128)(2,1)S(1)}, u32[]{:S(2)}, u32[]{:S(2)}) collective-permute-start(bf16[8,5,64,128]{3,2,1,0:T(8,128)(2,1)S(1)} %get-tuple-element.47), channel_id=1, source_target_pairs={{0,8},{4,12},{8,0},{12,4},{1,9},{5,13},{9,1},{13,5},{2,10},{6,14},... | collective-permute-start | bytes 1966088 | tf_op jit(solution)/shard_map/ppermute | solution.py:225
  265.5 89.2 %collective-permute-start.14 = (bf16[8,5,64,128]{3,2,1,0:T(8,128)(2,1)S(1)}, bf16[8,5,64,128]{3,2,1,0:T(8,128)(2,1)S(1)}, u32[]{:S(2)}, u32[]{:S(2)}) collective-permute-start(bf16[8,5,64,128]{3,2,1,0:T(8,128)(2,1)S(1)} %get-tuple-element.48), channel_id=1, source_target_pairs={{0,4},{4,8},{8,12},{12,0},{1,5},{5,9},{9,13},{13,1},{2,6},{6,10},{... | collective-permute-start | bytes 1966088 | tf_op jit(solution)/shard_map/ppermute | solution.py:225
  285.1 1.1 copy-start.7
  313.8 52.1 %collective-permute-start.18 = (bf16[8,5,64,128]{3,2,1,0:T(8,128)(2,1)S(1)}, bf16[8,5,64,128]{3,2,1,0:T(8,128)(2,1)S(1)}, u32[]{:S(2)}, u32[]{:S(2)}) collective-permute-start(bf16[8,5,64,128]{3,2,1,0:T(8,128)(2,1)S(1)} %get-tuple-element.52), channel_id=1, source_target_pairs={{0,12},{4,0},{8,4},{12,8},{1,13},{5,1},{9,5},{13,9},{2,14},{6,2},{... | collective-permute-start | bytes 1966088 | tf_op jit(solution)/shard_map/ppermute | solution.py:225
  350.7 54.0 %collective-permute-start.19 = (bf16[8,5,64,128]{3,2,1,0:T(8,128)(2,1)S(1)}, bf16[8,5,64,128]{3,2,1,0:T(8,128)(2,1)S(1)}, u32[]{:S(2)}, u32[]{:S(2)}) collective-permute-start(bf16[8,5,64,128]{3,2,1,0:T(8,128)(2,1)S(1)} %get-tuple-element.53), channel_id=1, source_target_pairs={{0,8},{4,12},{8,0},{12,4},{1,9},{5,13},{9,1},{13,5},{2,10},{6,14},... | collective-permute-start | bytes 1966088 | tf_op jit(solution)/shard_map/ppermute | solution.py:225
  350.7 54.0 %collective-permute-start.20 = (bf16[8,5,64,128]{3,2,1,0:T(8,128)(2,1)S(1)}, bf16[8,5,64,128]{3,2,1,0:T(8,128)(2,1)S(1)}, u32[]{:S(2)}, u32[]{:S(2)}) collective-permute-start(bf16[8,5,64,128]{3,2,1,0:T(8,128)(2,1)S(1)} %get-tuple-element.54), channel_id=1, source_target_pairs={{0,4},{4,8},{8,12},{12,0},{1,5},{5,9},{9,13},{13,1},{2,6},{6,10},{... | collective-permute-start | bytes 1966088 | tf_op jit(solution)/shard_map/ppermute | solution.py:225

commit v3 on v2

--- a/solution.py
+++ b/solution.py
@@ -35,29 +35,38 @@
     return pltpu.CompilerParams(vmem_limit_bytes=VMEM_BYTES, **more)
 
 
-def pack_kernel(splits, task_ref, q_ref, do_ref, *outs):
-    for part, ref in ((0, q_ref), (1, do_ref)):
-        flipped = jnp.swapaxes(ref[...].astype(F32), 0, 1).astype(BF16)
-        for (low, high), out in zip(splits, outs):
-            out[0, part] = flipped[low:high]
-
-
-def pack(queries, grad_out, task_of_slot, cube_len, far_count, splits):
-    _, heads, width = queries.shape
-    slots = task_of_slot.shape[0]
-    source = pl.BlockSpec((cube_len, heads, width), lambda s, t: (t[s] // far_count, 0, 0))
-    sizes = [(2, high - low, cube_len, width) for low, high in splits]
+def pack_kernel(steps, task_ref, *refs):
+    for step in range(steps):
+        refs[2 * steps + step][0, 0] = refs[step][...]
+        refs[2 * steps + step][0, 1] = refs[steps + step][...]
+
+
+def pack(q, do, task_of_slot, cube_len, far_count, steps, split):
+    low, high = split
+    heads, width = high - low, q.shape[2]
+    cap = task_of_slot.shape[0] // steps
+    block = low // heads
+    if low % heads:
+        q, do, block = q[low:high], do[low:high], 0
+
+    def source(step):
+        return pl.BlockSpec(
+            (heads, cube_len, width),
+            lambda s, t: (block, t[step * cap + s] // far_count, 0),
+        )
+
+    size = (2, heads, cube_len, width)
     return pl.pallas_call(
-        functools.partial(pack_kernel, splits),
+        functools.partial(pack_kernel, steps),
         grid_spec=pltpu.PrefetchScalarGridSpec(
             num_scalar_prefetch=1,
-            grid=(slots,),
-            in_specs=[source, source],
-            out_specs=[pl.BlockSpec((1,) + size, lambda s, t: (s, 0, 0, 0, 0)) for size in sizes],
-        ),
-        out_shape=[jax.ShapeDtypeStruct((slots,) + size, BF16) for size in sizes],
+            grid=(cap,),
+            in_specs=[source(step) for step in range(steps)] * 2,
+            out_specs=[pl.BlockSpec((1,) + size, lambda s, t: (s, 0, 0, 0, 0))] * steps,
+        ),
+        out_shape=[jax.ShapeDtypeStruct((cap,) + size, BF16)] * steps,
         compiler_params=params(),
-    )(task_of_slot, queries, grad_out)
+    )(task_of_slot, *([q] * steps), *([do] * steps))
 
 
 def near_kernel(
@@ -110,15 +119,12 @@
 
 def far_kernel(scaling, cap, steps, asked_ref, *refs):
     gots = refs[:steps]
-    stat_ref, k_ref, v_ref, nk_ref, nv_ref, ok_ref, ov_ref = refs[steps : steps + 7]
-    dqs = refs[steps + 7 : 2 * steps + 7]
-    gk_ref, gv_ref, acc_k, acc_v = refs[2 * steps + 7 :]
-    cubes, width = ok_ref.shape[1:]
-    cube_len = k_ref.shape[1] // cubes
-    for cube in range(cubes):
-        at = slice(cube * cube_len, (cube + 1) * cube_len)
-        acc_k[at, :] = nk_ref[0, at, :] + ok_ref[0, cube : cube + 1, :] * (1.0 / cube_len)
-        acc_v[at, :] = nv_ref[0, at, :] + ov_ref[0, cube : cube + 1, :] * (1.0 / cube_len)
+    stat_ref, k_ref, v_ref, nk_ref, nv_ref = refs[steps : steps + 5]
+    dqs = refs[steps + 6 : 2 * steps + 6]
+    acc_k, acc_v = refs[2 * steps + 6 :]
+    cube_len = gots[0].shape[3]
+    acc_k[...] = nk_ref[...]
+    acc_v[...] = nv_ref[...]
     for step in range(steps):
         pending = []
         for slot in range(cap):
@@ -136,20 +142,16 @@
             task_v = dot_nn(probs, do).astype(BF16)
             pending.append((at, task_k, task_v))
         for at, task_k, task_v in pending:
-            acc_k[at, :] += task_k.astype(F32)
-            acc_v[at, :] += task_v.astype(F32)
-    gk_ref[0] = acc_k[...].astype(BF16)
-    gv_ref[0] = acc_v[...].astype(BF16)
-
-
-def far(asked, gots, stats, k, v, near_k, near_v, own_k, own_v, low, scaling):
+            acc_k[0, at, :] += task_k.astype(F32)
+            acc_v[0, at, :] += task_v.astype(F32)
+
+
+def far(asked, gots, stats, k, v, near_k, near_v, after, low, scaling):
     steps = len(gots)
     cap, _, heads, cube_len, width = gots[0].shape
     slots = steps * cap
     rows = k.shape[1]
-    cubes = own_k.shape[1]
     token = pl.BlockSpec((1, rows, width), lambda h, a: (h + low, 0, 0))
-    cube = pl.BlockSpec((1, cubes, width), lambda h, a: (h + low, 0, 0))
     out = pl.BlockSpec((1, rows, width), lambda h, a: (h, 0, 0))
     got = pl.BlockSpec((cap, 2, 1, cube_len, width), lambda h, a: (0, 0, h, 0, 0))
     dq = pl.BlockSpec((cap, 1, cube_len, width), lambda h, a: (0, h, 0, 0))
@@ -161,19 +163,18 @@
             in_specs=[got] * steps
             + [pl.BlockSpec((1, slots, 2 * cube_len), lambda h, a: (h + low, 0, 0))]
             + [token] * 4
-            + [cube] * 2,
+            + [pl.BlockSpec(memory_space=pl.ANY)],
             out_specs=[dq] * steps + [out] * 2,
-            scratch_shapes=[pltpu.VMEM((rows, width), F32)] * 2,
         ),
         out_shape=[jax.ShapeDtypeStruct((cap, heads, cube_len, width), BF16)] * steps
-        + [jax.ShapeDtypeStruct((heads, rows, width), BF16)] * 2,
+        + [jax.ShapeDtypeStruct((heads, rows, width), F32)] * 2,
         compiler_params=params(),
         cost_estimate=pl.CostEstimate(
             flops=100 * heads * slots * cube_len * cube_len * width,
             bytes_accessed=heads * rows * width * 30,
             transcendentals=heads * slots * cube_len * cube_len,
         ),
-    )(asked, *gots, stats, k, v, near_k, near_v, own_k, own_v)
+    )(asked, *gots, stats, k, v, near_k, near_v, after)
     return results[:steps], results[steps], results[steps + 1]
 
 
@@ -181,7 +182,6 @@
     out = refs[-1]
     pieces = iter(refs[:-1])
     cube = pl.program_id(0)
-    total = []
     for low, high in splits:
         piece = nq_ref[low:high]
         for step in range(steps):
@@ -189,8 +189,7 @@
                 slot = slot_ref[cube * far_count + far_at]
                 here = (slot >= step * cap) & (slot < (step + 1) * cap)
                 piece = piece + jnp.where(here, next(pieces)[0].astype(F32), 0.0)
-        total.append(piece)
-    out[...] = jnp.swapaxes(jnp.concatenate(total, axis=0), 0, 1).astype(BF16)
+        out[low:high] = piece.astype(BF16)
 
 
 def join(near_q, back, slot_of_task, cube_len, far_count, splits):
@@ -213,9 +212,9 @@
             num_scalar_prefetch=1,
             grid=(rows // cube_len,),
             in_specs=[pl.BlockSpec((heads, cube_len, width), lambda c, s: (0, c, 0))] + specs,
-            out_specs=pl.BlockSpec((cube_len, heads, width), lambda c, s: (c, 0, 0)),
-        ),
-        out_shape=jax.ShapeDtypeStruct((rows, heads, width), BF16),
+            out_specs=pl.BlockSpec((heads, cube_len, width), lambda c, s: (0, c, 0)),
+        ),
+        out_shape=jax.ShapeDtypeStruct((heads, rows, width), BF16),
         compiler_params=params(),
     )(slot_of_task, near_q, *operands)
 
@@ -253,11 +252,16 @@
     def of_step(x, step):
         return x[step * cap : (step + 1) * cap]
 
-    sends = [
-        pack(queries, grad_out, of_step(task_of_slot, s), cube_len, far_count, splits)
-        for s in range(steps)
-    ]
-    first = [shift(sends[s][0], s + 1) for s in range(steps)]
+    def pack_half(split):
+        return pack(q, do, task_of_slot, cube_len, far_count, steps, split)
+
+    q, do = queries.transpose(1, 0, 2), grad_out.transpose(1, 0, 2)
+    sends = pack_half(splits[0])
+    sends, keys, values, fine_out, coarse_out, grad_out, q, do = lax.optimization_barrier(
+        (sends, keys, values, fine_out, coarse_out, grad_out, q, do)
+    )
+    first = [shift(sends[s], s + 1) for s in range(steps)]
+    later = pack_half(splits[1])
 
     def pooled(x):
         mean = jnp.mean(x.reshape(cubes, cube_len, heads, width), axis=1, dtype=F32)
@@ -284,7 +288,7 @@
     asked = got_stats[:, heads, 0].astype(jnp.int32)
     got_stats = got_stats[:, :heads].transpose(1, 0, 2)
 
-    q, do, k, v = (x.transpose(1, 0, 2) for x in (queries, grad_out, keys, values))
+    k, v = keys.transpose(1, 0, 2), values.transpose(1, 0, 2)
     stats = jnp.stack([fine_lse, delta_fine, coarse_lse, delta_coarse], axis=1)
     near_q, near_k, near_v, coarse_k, coarse_v = near(
         q, do, k, v, all_pooled[:heads], all_pooled[heads:], stats, scaling
@@ -293,24 +297,43 @@
     coarse = jnp.concatenate([coarse_k, coarse_v], axis=0)
     own = coarse[:, :cubes]
     for s in range(1, seq_size):
-        own = own + shift(coarse[:, s * cubes : (s + 1) * cubes], s)
+        piece = coarse[:, s * cubes : (s + 1) * cubes].astype(BF16)
+        own = own + shift(piece, s).astype(F32)
+
+    first, later, near_q, near_k, near_v = lax.optimization_barrier(
+        (first, later, near_q, near_k, near_v)
+    )
+    second = [shift(later[s], s + 1) for s in range(steps)]
+
+    def far_half(split, gots, after):
+        return far(asked, gots, got_stats, k, v, near_k, near_v, after, split[0], scaling)
+
+    def give_back(task_q):
+        return [shift(task_q[s], -(s + 1)) for s in range(steps)]
+
+    task_q, sum_k, sum_v = far_half(splits[0], first, first[0][0, 0, 0, :16])
+    task_q, second = lax.optimization_barrier((task_q, second))
+    back = [give_back(task_q)]
+    mark = shift(task_q[-1][0, 0, :16], 1)
+    sums_k, sums_v = [sum_k], [sum_v]
+    task_q, sum_k, sum_v = far_half(splits[1], second, mark)
+    back.append(give_back(task_q))
+    sums_k.append(sum_k)
+    sums_v.append(sum_v)
+
+    def with_pooled(sums, pooled_grad):
+        parts = []
+        for (low, high), part in zip(splits, sums):
+            spread = (pooled_grad[low:high] / cube_len)[:, :, None, :]
+            part = part.reshape(high - low, cubes, cube_len, width) + spread
+            parts.append(part.astype(BF16).reshape(high - low, rows, width))
+        return jnp.concatenate(parts, axis=0).transpose(1, 0, 2)
+
     own_k, own_v = own[:heads], own[heads:]
-
-    later = [send[1] for send in sends]
-    first, later = lax.optimization_barrier((first, later))
-    second = [shift(later[s], s + 1) for s in range(steps)]
-
-    back, grads_k, grads_v = [], [], []
-    for (low, high), gots in zip(splits, (first, second)):
-        task_q, grad_k, grad_v = far(
-            asked, gots, got_stats, k, v, near_k, near_v, own_k, own_v, low, scaling
-        )
-        back.append([shift(task_q[s], -(s + 1)) for s in range(steps)])
-        grads_k.append(grad_k)
-        grads_v.append(grad_v)
+    grad_keys = with_pooled(sums_k, own_k)
+    grad_values = with_pooled(sums_v, own_v)
     grad_queries = join(near_q, back, slot_of_task, cube_len, far_count, splits)
-    grad_keys = jnp.concatenate(grads_k, axis=0).transpose(1, 0, 2)
-    grad_values = jnp.concatenate(grads_v, axis=0).transpose(1, 0, 2)
+    grad_queries = grad_queries.transpose(1, 0, 2)
     return (
         grad_queries,
         grad_keys,

time: 423 us -> 399 us (0.943)
  waiting for transfers between devices: 140 us -> 125 us
  local copies, waits for them, and re-layouts: 17.3 us -> 5.44 us
  starting transfers between devices: 123 us -> 132 us
    ppermute x21 -> x22, waiting for transfers between devices: 140 us -> 125 us  [shift(): return lax.ppermute(x, 'seq', [(i, (i + step) % size) for i in range(size)])]
    unnamed x22 -> x29, local copies, waits for them, and re-layouts: 13.2 us -> 2.22 us
    ppermute x21 -> x22, starting transfers between devices: 123 us -> 132 us  [shift(): return lax.ppermute(x, 'seq', [(i, (i + step) % size) for i in range(size)])]
    pallas_call x3 -> x2, Pallas kernels: 15.8 us -> 13 us  [pack(): pl.pallas_call(functools.partial(pack_kernel, steps), grid_spec=pltpu.Pre...]
  transfers between devices with their start and end apart: 21 -> 22, of which waited for: 4 -> 8; matrix products, arithmetic and copies ran while one was open for 5% -> 3% of each run, Pallas kernels for 27% -> 26%
where the time goes in v3:
time: 399 us; the launch traced here: 398 us
  starting transfers between devices  132 us (33%)
  waiting for transfers between devices  125 us (31%)
  Pallas kernels  122 us (31%)
  other arithmetic  13.1 us (3%)
  local copies, waits for them, and re-layouts  5.44 us (1%)
    ppermute x22, starting transfers between devices, shift(): return lax.ppermute(x, 'seq', [(i, (i + step) % size) for i in range(size)])  132 us
    ppermute x22, waiting for transfers between devices, shift(): return lax.ppermute(x, 'seq', [(i, (i + step) % size) for i in range(size)])  125 us
    pallas_call x2, Pallas kernels, far(): pl.pallas_call(functools.partial(far_kernel, scaling, cap, steps), grid_s...  57.3 us
    pallas_call x1, Pallas kernels, near(): pl.pallas_call(functools.partial(near_kernel, scaling, min(256, rows)), g...  40.7 us
    pallas_call x2, Pallas kernels, pack(): pl.pallas_call(functools.partial(pack_kernel, steps), grid_spec=pltpu.Pre...  13 us
    pallas_call x1, Pallas kernels, join(): pl.pallas_call(functools.partial(join_kernel, splits, steps, cap, far_cou...  11.2 us
  transfers between devices with their start and end apart: 22, of which 8 were waited for; matrix products, arithmetic and copies ran while one was open for 3% of the time, Pallas kernels for 26%

profile of v3, /device:TPU:0, one launch (start us, length us, event | category | flops | bytes accessed | tf_op | source)
XLA Modules:
  0.0 398.4 jit_solution(9387063716006232127)
XLA Ops:
  2.3 6.2 %shard_map.128 = (bf16[8,2,5,64,128]{4,3,2,1,0:T(8,128)(2,1)S(1)}, bf16[8,2,5,64,128]{4,3,2,1,0:T(8,128)(2,1)S(1)}, bf16[8,2,5,64,128]{4,3,2,1,0:T(8,128)(2,1)S(1)}) custom-call(s32[24]{0:T(128)S(1)} %get-tuple-element.100.task_ref, bf16[10,1024,128]{2,1,0:T(8,128)(2,1)} %bitcast.82, bf16[10,1024,128]{2,1,0:T(8,128)(2,1)} %bitcast.83, ...), custom_call_target="tpu_custom_call" | custom-call | tf_op jit(solution)/shard_map/pallas_call | solution.py:59
  8.6 2.1 convert_reduce_fusion
  11.4 5.1 %collective-permute-start.3 = (bf16[20,16,128]{2,1,0:T(8,128)(2,1)}, bf16[20,16,128]{2,1,0:T(8,128)(2,1)S(1)}, u32[]{:S(2)}, u32[]{:S(2)}) collective-permute-start(bf16[20,16,128]{2,1,0:T(8,128)(2,1)} %pad_maximum_fusion.3), channel_id=1, source_target_pairs={{0,12},{4,0},{8,4},{12,8},{1,13},{5,1},{9,5},{13,9},{2,14},{6,2},{... | collective-permute-start | bytes 245768 | tf_op jit(solution)/shard_map/ppermute | solution.py:224
  16.5 1.1 collective-permute-start.5
  17.6 2.8 fusion
  22.2 2.5 collective-permute-start.6
  26.8 6.8 %shard_map.129 = (bf16[8,2,5,64,128]{4,3,2,1,0:T(8,128)(2,1)S(1)}, bf16[8,2,5,64,128]{4,3,2,1,0:T(8,128)(2,1)}, bf16[8,2,5,64,128]{4,3,2,1,0:T(8,128)(2,1)S(1)}) custom-call(s32[24]{0:T(128)S(1)} %get-tuple-element.100.task_ref, bf16[10,1024,128]{2,1,0:T(8,128)(2,1)} %bitcast.85, bf16[10,1024,128]{2,1,0:T(8,128)(2,1)} %bitcast.86, ...), custom_call_target="tpu_custom_call" | custom-call | tf_op jit(solution)/shard_map/pallas_call | solution.py:59
  33.5 1.6 collective-permute-start.8
  35.7 1.9 collective-permute-done.8
  37.6 2.5 collective-permute-start.1
  40.1 1.8 collective-permute-start.2
  42.9 40.7 %shard_map.130 = (f32[10,1024,128]{2,1,0:T(8,128)}, f32[10,1024,128]{2,1,0:T(8,128)}, f32[10,1024,128]{2,1,0:T(8,128)}, f32[10,64,128]{2,1,0:T(8,128)S(1)}, f32[10,64,128]{2,1,0:T(8,128)S(1)}) custom-call(bf16[10,1024,128]{2,1,0:T(8,128)(2,1)S(1)} %bitcast.88, bf16[10,1024,128]{2,1,0:T(8,128)(2,1)} %bitcast.95, bf16[10,1024,128]{2,1,0:T(8,128)(2,1)} %bitcast.96, ...), custom_call_target="tpu_custom_call" | custom-call | flops 28521267200 | bytes 26214400 | tf_op jit(solution)/shard_map/pallas_call | solution.py:105
  83.7 39.1 %collective-permute-done.1.refs_1_ = bf16[8,2,5,64,128]{4,3,2,1,0:T(8,128)(2,1)S(1)} collective-permute-done((bf16[8,2,5,64,128]{4,3,2,1,0:T(8,128)(2,1)S(1)}, bf16[8,2,5,64,128]{4,3,2,1,0:T(8,128)(2,1)S(1)}, u32[]{:S(2)}, u32[]{:S(2)}) %collective-permute-start.1) | collective-permute-done | bytes 1310752 | tf_op jit(solution)/shard_map/ppermute | solution.py:224
  122.8 27.3 %collective-permute-start.10 = (bf16[8,2,5,64,128]{4,3,2,1,0:T(8,128)(2,1)}, bf16[8,2,5,64,128]{4,3,2,1,0:T(8,128)(2,1)S(1)}, u32[]{:S(2)}, u32[]{:S(2)}) collective-permute-start(bf16[8,2,5,64,128]{4,3,2,1,0:T(8,128)(2,1)} %get-tuple-element.80), channel_id=1, source_target_pairs={{0,8},{4,12},{8,0},{12,4},{1,9},{5,13},{9,1},{13,5},{2,10},{6,14},... | collective-permute-start | bytes 3932168 | tf_op jit(solution)/shard_map/ppermute | solution.py:224
  150.1 3.5 collective-permute-start.11
  154.3 4.2 %collective-permute-start.20 = (bf16[20,16,128]{2,1,0:T(8,128)(2,1)S(1)}, bf16[20,16,128]{2,1,0:T(8,128)(2,1)S(1)}, u32[]{:S(2)}, u32[]{:S(2)}) collective-permute-start(bf16[20,16,128]{2,1,0:T(8,128)(2,1)S(1)} %get-tuple-element.103), channel_id=1, source_target_pairs={{0,8},{4,12},{8,0},{12,4},{1,9},{5,13},{9,1},{13,5},{2,10},{6,14},... | collective-permute-start | bytes 245768 | tf_op jit(solution)/shard_map/ppermute | solution.py:224
  158.5 28.7 %shard_map.131 = (bf16[8,5,64,128]{3,2,1,0:T(8,128)(2,1)}, bf16[8,5,64,128]{3,2,1,0:T(8,128)(2,1)S(1)}, bf16[8,5,64,128]{3,2,1,0:T(8,128)(2,1)S(1)}, f32[5,1024,128]{2,1,0:T(8,128)}, f32[5,1024,128]{2,1,0:T(8,128)}) custom-call(s32[24]{0:T(128)S(1)} %fusion.10.asked_ref, bf16[8,2,5,64,128]{4,3,2,1,0:T(8,128)(2,1)S(1)} %collective-permute-done.refs_0_, ...), custom_call_target="tpu_custom_call" | custom-call | flops 6291456000 | bytes 19660800 | tf_op jit(solution)/shard_map/pallas_call | solution.py:158
  187.1 20.9 %collective-permute-done.10.refs_1_ = bf16[8,2,5,64,128]{4,3,2,1,0:T(8,128)(2,1)S(1)} collective-permute-done((bf16[8,2,5,64,128]{4,3,2,1,0:T(8,128)(2,1)}, bf16[8,2,5,64,128]{4,3,2,1,0:T(8,128)(2,1)S(1)}, u32[]{:S(2)}, u32[]{:S(2)}) %collective-permute-start.10) | collective-permute-done | bytes 1310752 | tf_op jit(solution)/shard_map/ppermute | solution.py:224
  208.0 30.8 %collective-permute-start.21 = (bf16[20,16,128]{2,1,0:T(8,128)(2,1)S(1)}, bf16[20,16,128]{2,1,0:T(8,128)(2,1)S(1)}, u32[]{:S(2)}, u32[]{:S(2)}) collective-permute-start(bf16[20,16,128]{2,1,0:T(8,128)(2,1)S(1)} %get-tuple-element.102), channel_id=1, source_target_pairs={{0,12},{4,0},{8,4},{12,8},{1,13},{5,1},{9,5},{13,9},{2,14},{6,2},{... | collective-permute-start | bytes 245768 | tf_op jit(solution)/shard_map/ppermute | solution.py:224
  239.8 28.6 %collective-permute-start.15 = (bf16[16,128]{1,0:T(8,128)(2,1)S(1)}, bf16[16,128]{1,0:T(8,128)(2,1)S(1)}, u32[]{:S(2)}, u32[]{:S(2)}) collective-permute-start(bf16[16,128]{1,0:T(8,128)(2,1)S(1)} %slice_bitcast_fusion.3), channel_id=1, source_target_pairs={{0,4},{4,8},{8,12},{12,0},{1,5},{5,9},{9,13},{13,1},{2,6},{6,10},{... | collective-permute-start | bytes 12296 | tf_op jit(solution)/shard_map/ppermute | solution.py:224
  268.4 1.2 collective-permute-done.20
  269.6 15.6 %collective-permute-start.14 = (bf16[8,5,64,128]{3,2,1,0:T(8,128)(2,1)S(1)}, bf16[8,5,64,128]{3,2,1,0:T(8,128)(2,1)S(1)}, u32[]{:S(2)}, u32[]{:S(2)}) collective-permute-start(bf16[8,5,64,128]{3,2,1,0:T(8,128)(2,1)S(1)} %get-tuple-element.84), channel_id=1, source_target_pairs={{0,4},{4,8},{8,12},{12,0},{1,5},{5,9},{9,13},{13,1},{2,6},{6,10},{... | collective-permute-start | bytes 1966088 | tf_op jit(solution)/shard_map/ppermute | solution.py:224
  285.2 3.4 collective-permute-start.13
  288.6 28.6 %shard_map.132 = (bf16[8,5,64,128]{3,2,1,0:T(8,128)(2,1)S(1)}, bf16[8,5,64,128]{3,2,1,0:T(8,128)(2,1)S(1)}, bf16[8,5,64,128]{3,2,1,0:T(8,128)(2,1)S(1)}, f32[5,1024,128]{2,1,0:T(8,128)}, f32[5,1024,128]{2,1,0:T(8,128)}) custom-call(s32[24]{0:T(128)S(1)} %fusion.10.asked_ref, bf16[8,2,5,64,128]{4,3,2,1,0:T(8,128)(2,1)S(1)} %collective-permute-done.9.refs_0_, ...), custom_call_target="tpu_custom_call" | custom-call | flops 6291456000 | bytes 19660800 | tf_op jit(solution)/shard_map/pallas_call | solution.py:158
  317.2 1.5 collective-permute-start.17
  320.4 1.5 copy-done.11
  323.0 1.7 maximum_bitcast_fusion.1
  324.7 1.7 maximum_bitcast_fusion
  326.4 4.7 %collective-permute-done.13.refs_1_ = bf16[8,5,64,128]{3,2,1,0:T(8,128)(2,1)S(1)} collective-permute-done((bf16[8,5,64,128]{3,2,1,0:T(8,128)(2,1)S(1)}, bf16[8,5,64,128]{3,2,1,0:T(8,128)(2,1)S(1)}, u32[]{:S(2)}, u32[]{:S(2)}) %collective-permute-start.13) | collective-permute-done | bytes 655392 | tf_op jit(solution)/shard_map/ppermute | solution.py:224
  331.1 13.9 %collective-permute-done.16.refs_3_ = bf16[8,5,64,128]{3,2,1,0:T(8,128)(2,1)S(1)} collective-permute-done((bf16[8,5,64,128]{3,2,1,0:T(8,128)(2,1)S(1)}, bf16[8,5,64,128]{3,2,1,0:T(8,128)(2,1)S(1)}, u32[]{:S(2)}, u32[]{:S(2)}) %collective-permute-start.16) | collective-permute-done | bytes 655392 | tf_op jit(solution)/shard_map/ppermute | solution.py:224
  345.0 42.2 %collective-permute-done.17.refs_4_ = bf16[8,5,64,128]{3,2,1,0:T(8,128)(2,1)S(1)} collective-permute-done((bf16[8,5,64,128]{3,2,1,0:T(8,128)(2,1)S(1)}, bf16[8,5,64,128]{3,2,1,0:T(8,128)(2,1)S(1)}, u32[]{:S(2)}, u32[]{:S(2)}) %collective-permute-start.17) | collective-permute-done | bytes 655392 | tf_op jit(solution)/shard_map/ppermute | solution.py:224
  387.2 11.2 %shard_map.133 = bf16[10,1024,128]{2,1,0:T(8,128)(2,1)} custom-call(s32[16]{0:T(128)S(1)} %multiply_add_fusion.slot_ref, f32[10,1024,128]{2,1,0:T(8,128)} %get-tuple-element.70.nq_ref, bf16[8,5,64,128]{3,2,1,0:T(8,128)(2,1)S(1)} %collective-permute-done.12.refs_0_, bf16[8,5,64,128]{3,2,1,0:T(8,128)(2,1)S(1)} %collective-permute-done.13.refs_1_, ...), custom_call_target="tpu_custom_call" | custom-call | tf_op jit(solution)/shard_map/pallas_call | solution.py:209
  (96 shorter events, 11.9 us)
Async XLA Ops:
  2.3 6.2 %copy-start.6 = (bf16[1024,10,128]{2,0,1:T(8,128)(2,1)S(1)}, bf16[1024,10,128]{2,0,1:T(8,128)(2,1)}, u32[]{:S(2)}) copy-start(bf16[1024,10,128]{2,0,1:T(8,128)(2,1)} %param.10) | copy-start | bytes 7864324
  2.3 6.2 %copy-start.7 = (bf16[1024,10,128]{2,0,1:T(8,128)(2,1)S(1)}, bf16[1024,10,128]{2,0,1:T(8,128)(2,1)}, u32[]{:S(2)}) copy-start(bf16[1024,10,128]{2,0,1:T(8,128)(2,1)} %param.11) | copy-start | bytes 7864324
  2.3 15.3 %copy-start.5 = (bf16[1024,10,128]{2,0,1:T(8,128)(2,1)S(1)}, bf16[1024,10,128]{2,0,1:T(8,128)(2,1)}, u32[]{:S(2)}) copy-start(bf16[1024,10,128]{2,0,1:T(8,128)(2,1)} %param.14) | copy-start | bytes 7864324
  8.5 9.1 %copy-start.3 = (bf16[1024,10,128]{2,0,1:T(8,128)(2,1)S(1)}, bf16[1024,10,128]{2,0,1:T(8,128)(2,1)}, u32[]{:S(2)}) copy-start(bf16[1024,10,128]{2,0,1:T(8,128)(2,1)} %param.12) | copy-start | bytes 7864324
  8.5 9.1 %copy-start.4 = (bf16[1024,10,128]{2,0,1:T(8,128)(2,1)S(1)}, bf16[1024,10,128]{2,0,1:T(8,128)(2,1)}, u32[]{:S(2)}) copy-start(bf16[1024,10,128]{2,0,1:T(8,128)(2,1)} %param.13) | copy-start | bytes 7864324
  11.4 28.7 %collective-permute-start.3 = (bf16[20,16,128]{2,1,0:T(8,128)(2,1)}, bf16[20,16,128]{2,1,0:T(8,128)(2,1)S(1)}, u32[]{:S(2)}, u32[]{:S(2)}) collective-permute-start(bf16[20,16,128]{2,1,0:T(8,128)(2,1)} %pad_maximum_fusion.3), channel_id=1, source_target_pairs={{0,12},{4,0},{8,4},{12,8},{1,13},{5,1},{9,5},{13,9},{2,14},{6,2},{... | collective-permute-start | bytes 245768 | tf_op jit(solution)/shard_map/ppermute | solution.py:224
  16.5 25.5 %collective-permute-start.4 = (bf16[20,16,128]{2,1,0:T(8,128)(2,1)}, bf16[20,16,128]{2,1,0:T(8,128)(2,1)S(1)}, u32[]{:S(2)}, u32[]{:S(2)}) collective-permute-start(bf16[20,16,128]{2,1,0:T(8,128)(2,1)} %pad_maximum_fusion.3), channel_id=1, source_target_pairs={{0,8},{4,12},{8,0},{12,4},{1,9},{5,13},{9,1},{13,5},{2,10},{6,14},... | collective-permute-start | bytes 245768 | tf_op jit(solution)/shard_map/ppermute | solution.py:224
  16.5 25.5 %collective-permute-start.5 = (bf16[20,16,128]{2,1,0:T(8,128)(2,1)}, bf16[20,16,128]{2,1,0:T(8,128)(2,1)}, u32[]{:S(2)}, u32[]{:S(2)}) collective-permute-start(bf16[20,16,128]{2,1,0:T(8,128)(2,1)} %pad_maximum_fusion.3), channel_id=1, source_target_pairs={{0,4},{4,8},{8,12},{12,0},{1,5},{5,9},{9,13},{13,1},{2,6},{6,10},{... | collective-permute-start | bytes 245768 | tf_op jit(solution)/shard_map/ppermute | solution.py:224
  17.6 3.6 copy-start.12
  22.2 11.3 %collective-permute-start.6 = (f32[8,11,128]{2,0,1:T(8,128)S(1)}, f32[8,11,128]{2,0,1:T(8,128)S(1)}, u32[]{:S(2)}, u32[]{:S(2)}) collective-permute-start(f32[8,11,128]{2,0,1:T(8,128)S(1)} %get-tuple-element.114), channel_id=1, source_target_pairs={{0,4},{4,8},{8,12},{12,0},{1,5},{5,9},{9,13},{13,1},{2,6},{6,10},{... | collective-permute-start | bytes 135176 | tf_op jit(solution)/shard_map/ppermute | solution.py:224
  24.7 10.4 %collective-permute-start.7 = (f32[8,11,128]{2,0,1:T(8,128)S(1)}, f32[8,11,128]{2,0,1:T(8,128)S(1)}, u32[]{:S(2)}, u32[]{:S(2)}) collective-permute-start(f32[8,11,128]{2,0,1:T(8,128)S(1)} %get-tuple-element.113), channel_id=1, source_target_pairs={{0,8},{4,12},{8,0},{12,4},{1,9},{5,13},{9,1},{13,5},{2,10},{6,14},... | collective-permute-start | bytes 135176 | tf_op jit(solution)/shard_map/ppermute | solution.py:224
  26.7 8.4 %copy-start.2 = (bf16[8,2,5,64,128]{4,3,2,1,0:T(8,128)(2,1)S(1)}, bf16[8,2,5,64,128]{4,3,2,1,0:T(8,128)(2,1)}, u32[]{:S(2)}) copy-start(bf16[8,2,5,64,128]{4,3,2,1,0:T(8,128)(2,1)} %copy-done.1) | copy-start | bytes 3932164
  26.8 16.2 %copy-start = (bf16[1024,10,128]{2,0,1:T(8,128)(2,1)S(1)}, bf16[1024,10,128]{2,0,1:T(8,128)(2,1)}, u32[]{:S(2)}) copy-start(bf16[1024,10,128]{2,0,1:T(8,128)(2,1)} %param.9) | copy-start | bytes 7864324
  33.5 4.1 %collective-permute-start.8 = (f32[8,11,128]{2,0,1:T(8,128)S(1)}, f32[8,11,128]{2,0,1:T(8,128)S(1)}, u32[]{:S(2)}, u32[]{:S(2)}) collective-permute-start(f32[8,11,128]{2,0,1:T(8,128)S(1)} %get-tuple-element.112), channel_id=1, source_target_pairs={{0,12},{4,0},{8,4},{12,8},{1,13},{5,1},{9,5},{13,9},{2,14},{6,2},{... | collective-permute-start | bytes 135176 | tf_op jit(solution)/shard_map/ppermute | solution.py:224
  35.1 48.5 %collective-permute-start = (bf16[8,2,5,64,128]{4,3,2,1,0:T(8,128)(2,1)S(1)}, bf16[8,2,5,64,128]{4,3,2,1,0:T(8,128)(2,1)S(1)}, u32[]{:S(2)}, u32[]{:S(2)}) collective-permute-start(bf16[8,2,5,64,128]{4,3,2,1,0:T(8,128)(2,1)S(1)} %copy-done.2), channel_id=1, source_target_pairs={{0,4},{4,8},{8,12},{12,0},{1,5},{5,9},{9,13},{13,1},{2,6},{6,10},{... | collective-permute-start | bytes 3932168 | tf_op jit(solution)/shard_map/ppermute | solution.py:224
  37.6 85.2 %collective-permute-start.1 = (bf16[8,2,5,64,128]{4,3,2,1,0:T(8,128)(2,1)S(1)}, bf16[8,2,5,64,128]{4,3,2,1,0:T(8,128)(2,1)S(1)}, u32[]{:S(2)}, u32[]{:S(2)}) collective-permute-start(bf16[8,2,5,64,128]{4,3,2,1,0:T(8,128)(2,1)S(1)} %get-tuple-element.55), channel_id=1, source_target_pairs={{0,8},{4,12},{8,0},{12,4},{1,9},{5,13},{9,1},{13,5},{2,10},{6,14},... | collective-permute-start | bytes 3932168 | tf_op jit(solution)/shard_map/ppermute | solution.py:224
  40.1 82.7 %collective-permute-start.2 = (bf16[8,2,5,64,128]{4,3,2,1,0:T(8,128)(2,1)S(1)}, bf16[8,2,5,64,128]{4,3,2,1,0:T(8,128)(2,1)}, u32[]{:S(2)}, u32[]{:S(2)}) collective-permute-start(bf16[8,2,5,64,128]{4,3,2,1,0:T(8,128)(2,1)S(1)} %get-tuple-element.56), channel_id=1, source_target_pairs={{0,12},{4,0},{8,4},{12,8},{1,13},{5,1},{9,5},{13,9},{2,14},{6,2},{... | collective-permute-start | bytes 3932168 | tf_op jit(solution)/shard_map/ppermute | solution.py:224
  122.8 85.2 %collective-permute-start.10 = (bf16[8,2,5,64,128]{4,3,2,1,0:T(8,128)(2,1)}, bf16[8,2,5,64,128]{4,3,2,1,0:T(8,128)(2,1)S(1)}, u32[]{:S(2)}, u32[]{:S(2)}) collective-permute-start(bf16[8,2,5,64,128]{4,3,2,1,0:T(8,128)(2,1)} %get-tuple-element.80), channel_id=1, source_target_pairs={{0,8},{4,12},{8,0},{12,4},{1,9},{5,13},{9,1},{13,5},{2,10},{6,14},... | collective-permute-start | bytes 3932168 | tf_op jit(solution)/shard_map/ppermute | solution.py:224
  150.1 88.8 %collective-permute-start.11 = (bf16[8,2,5,64,128]{4,3,2,1,0:T(8,128)(2,1)S(1)}, bf16[8,2,5,64,128]{4,3,2,1,0:T(8,128)(2,1)S(1)}, u32[]{:S(2)}, u32[]{:S(2)}) collective-permute-start(bf16[8,2,5,64,128]{4,3,2,1,0:T(8,128)(2,1)S(1)} %get-tuple-element.81), channel_id=1, source_target_pairs={{0,12},{4,0},{8,4},{12,8},{1,13},{5,1},{9,5},{13,9},{2,14},{6,2},{... | collective-permute-start | bytes 3932168 | tf_op jit(solution)/shard_map/ppermute | solution.py:224
  153.6 86.2 %collective-permute-start.9 = (bf16[8,2,5,64,128]{4,3,2,1,0:T(8,128)(2,1)S(1)}, bf16[8,2,5,64,128]{4,3,2,1,0:T(8,128)(2,1)S(1)}, u32[]{:S(2)}, u32[]{:S(2)}) collective-permute-start(bf16[8,2,5,64,128]{4,3,2,1,0:T(8,128)(2,1)S(1)} %get-tuple-element.79), channel_id=1, source_target_pairs={{0,4},{4,8},{8,12},{12,0},{1,5},{5,9},{9,13},{13,1},{2,6},{6,10},{... | collective-permute-start | bytes 3932168 | tf_op jit(solution)/shard_map/ppermute | solution.py:224
  153.8 114.6 %collective-permute-start.19 = (bf16[20,16,128]{2,1,0:T(8,128)(2,1)S(1)}, bf16[20,16,128]{2,1,0:T(8,128)(2,1)S(1)}, u32[]{:S(2)}, u32[]{:S(2)}) collective-permute-start(bf16[20,16,128]{2,1,0:T(8,128)(2,1)S(1)} %get-tuple-element.101), channel_id=1, source_target_pairs={{0,4},{4,8},{8,12},{12,0},{1,5},{5,9},{9,13},{13,1},{2,6},{6,10},{... | collective-permute-start | bytes 245768 | tf_op jit(solution)/shard_map/ppermute | solution.py:224
  154.3 115.3 %collective-permute-start.20 = (bf16[20,16,128]{2,1,0:T(8,128)(2,1)S(1)}, bf16[20,16,128]{2,1,0:T(8,128)(2,1)S(1)}, u32[]{:S(2)}, u32[]{:S(2)}) collective-permute-start(bf16[20,16,128]{2,1,0:T(8,128)(2,1)S(1)} %get-tuple-element.103), channel_id=1, source_target_pairs={{0,8},{4,12},{8,0},{12,4},{1,9},{5,13},{9,1},{13,5},{2,10},{6,14},... | collective-permute-start | bytes 245768 | tf_op jit(solution)/shard_map/ppermute | solution.py:224
  208.0 61.5 %collective-permute-start.21 = (bf16[20,16,128]{2,1,0:T(8,128)(2,1)S(1)}, bf16[20,16,128]{2,1,0:T(8,128)(2,1)S(1)}, u32[]{:S(2)}, u32[]{:S(2)}) collective-permute-start(bf16[20,16,128]{2,1,0:T(8,128)(2,1)S(1)} %get-tuple-element.102), channel_id=1, source_target_pairs={{0,12},{4,0},{8,4},{12,8},{1,13},{5,1},{9,5},{13,9},{2,14},{6,2},{... | collective-permute-start | bytes 245768 | tf_op jit(solution)/shard_map/ppermute | solution.py:224
  239.8 48.8 %collective-permute-start.15 = (bf16[16,128]{1,0:T(8,128)(2,1)S(1)}, bf16[16,128]{1,0:T(8,128)(2,1)S(1)}, u32[]{:S(2)}, u32[]{:S(2)}) collective-permute-start(bf16[16,128]{1,0:T(8,128)(2,1)S(1)} %slice_bitcast_fusion.3), channel_id=1, source_target_pairs={{0,4},{4,8},{8,12},{12,0},{1,5},{5,9},{9,13},{13,1},{2,6},{6,10},{... | collective-permute-start | bytes 12296 | tf_op jit(solution)/shard_map/ppermute | solution.py:224
  268.4 50.4 %collective-permute-start.12 = (bf16[8,5,64,128]{3,2,1,0:T(8,128)(2,1)}, bf16[8,5,64,128]{3,2,1,0:T(8,128)(2,1)S(1)}, u32[]{:S(2)}, u32[]{:S(2)}) collective-permute-start(bf16[8,5,64,128]{3,2,1,0:T(8,128)(2,1)} %get-tuple-element.82), channel_id=1, source_target_pairs={{0,12},{4,0},{8,4},{12,8},{1,13},{5,1},{9,5},{13,9},{2,14},{6,2},{... | collective-permute-start | bytes 1966088 | tf_op jit(solution)/shard_map/ppermute | solution.py:224
  269.6 50.4 %copy-start.9 = (f32[5,1024,128]{2,1,0:T(8,128)S(1)}, f32[5,1024,128]{2,1,0:T(8,128)}, u32[]{:S(2)}) copy-start(f32[5,1024,128]{2,1,0:T(8,128)} %get-tuple-element.95) | copy-start | bytes 7864324
  269.6 61.5 %collective-permute-start.14 = (bf16[8,5,64,128]{3,2,1,0:T(8,128)(2,1)S(1)}, bf16[8,5,64,128]{3,2,1,0:T(8,128)(2,1)S(1)}, u32[]{:S(2)}, u32[]{:S(2)}) collective-permute-start(bf16[8,5,64,128]{3,2,1,0:T(8,128)(2,1)S(1)} %get-tuple-element.84), channel_id=1, source_target_pairs={{0,4},{4,8},{8,12},{12,0},{1,5},{5,9},{9,13},{13,1},{2,6},{6,10},{... | collective-permute-start | bytes 1966088 | tf_op jit(solution)/shard_map/ppermute | solution.py:224
  285.2 45.9 %collective-permute-start.13 = (bf16[8,5,64,128]{3,2,1,0:T(8,128)(2,1)S(1)}, bf16[8,5,64,128]{3,2,1,0:T(8,128)(2,1)S(1)}, u32[]{:S(2)}, u32[]{:S(2)}) collective-permute-start(bf16[8,5,64,128]{3,2,1,0:T(8,128)(2,1)S(1)} %get-tuple-element.83), channel_id=1, source_target_pairs={{0,8},{4,12},{8,0},{12,4},{1,9},{5,13},{9,1},{13,5},{2,10},{6,14},... | collective-permute-start | bytes 1966088 | tf_op jit(solution)/shard_map/ppermute | solution.py:224
  317.2 3.0 copy-start.8
  317.2 27.7 %collective-permute-start.16 = (bf16[8,5,64,128]{3,2,1,0:T(8,128)(2,1)S(1)}, bf16[8,5,64,128]{3,2,1,0:T(8,128)(2,1)S(1)}, u32[]{:S(2)}, u32[]{:S(2)}) collective-permute-start(bf16[8,5,64,128]{3,2,1,0:T(8,128)(2,1)S(1)} %get-tuple-element.88), channel_id=1, source_target_pairs={{0,12},{4,0},{8,4},{12,8},{1,13},{5,1},{9,5},{13,9},{2,14},{6,2},{... | collective-permute-start | bytes 1966088 | tf_op jit(solution)/shard_map/ppermute | solution.py:224
  317.2 69.9 %collective-permute-start.17 = (bf16[8,5,64,128]{3,2,1,0:T(8,128)(2,1)S(1)}, bf16[8,5,64,128]{3,2,1,0:T(8,128)(2,1)S(1)}, u32[]{:S(2)}, u32[]{:S(2)}) collective-permute-start(bf16[8,5,64,128]{3,2,1,0:T(8,128)(2,1)S(1)} %get-tuple-element.89), channel_id=1, source_target_pairs={{0,8},{4,12},{8,0},{12,4},{1,9},{5,13},{9,1},{13,5},{2,10},{6,14},... | collective-permute-start | bytes 1966088 | tf_op jit(solution)/shard_map/ppermute | solution.py:224
  318.8 68.4 %collective-permute-start.18 = (bf16[8,5,64,128]{3,2,1,0:T(8,128)(2,1)S(1)}, bf16[8,5,64,128]{3,2,1,0:T(8,128)(2,1)S(1)}, u32[]{:S(2)}, u32[]{:S(2)}) collective-permute-start(bf16[8,5,64,128]{3,2,1,0:T(8,128)(2,1)S(1)} %get-tuple-element.90), channel_id=1, source_target_pairs={{0,4},{4,8},{8,12},{12,0},{1,5},{5,9},{9,13},{13,1},{2,6},{6,10},{... | collective-permute-start | bytes 1966088 | tf_op jit(solution)/shard_map/ppermute | solution.py:224
  (3 other events, 6.3 us)
